TPU v7x, 32 devices: a whole 2x2x4 slice. The times are simulated.
32 devices in a mesh: fsdp: 2 (over core), ctx: 4 (over z), tp: 4 (over y, x).
Axes of the slice: x: 2, y: 2, z: 4, core: 2. Of those that a mesh axis runs over, the one named last changes fastest.
Arguments:
- tokens: bfloat16 [4096, 2048], P(('fsdp', 'ctx')), may hold values from -6 to 6
- seq_bounds: int32 [2, 3], P('fsdp'), may hold values from 0 to 2048, as said below
- w_query: bfloat16 [2048, 2048], P('fsdp', 'tp'), may hold values from -0.125 to 0.125
- w_key: bfloat16 [2048, 2048], P('fsdp', 'tp'), may hold values from -0.125 to 0.125
- w_value: bfloat16 [2048, 2048], P('fsdp', 'tp'), may hold values from -0.125 to 0.125
- w_beta: bfloat16 [2048, 16], P('fsdp', 'tp'), may hold values from -0.125 to 0.125
- conv_taps: float32 [3, 4, 2048], P(None, None, 'tp'), may hold values from -3 to 3
- out_gain: float32 [128], replicated, may hold values from 0.1 to 1.9
- w_out: bfloat16 [2048, 2048], P('fsdp', 'tp'), may hold values from -0.125 to 0.125
- attn_gain: float32 [2048], replicated, may hold values from 0.1 to 1.9
- ffn_gain: float32 [2048], replicated, may hold values from 0.1 to 1.9
- w_gate: bfloat16 [2048, 5632], P('fsdp', 'tp'), may hold values from -0.125 to 0.125
- w_up: bfloat16 [2048, 5632], P('fsdp', 'tp'), may hold values from -0.125 to 0.125
- w_down: bfloat16 [2048, 5632], P('fsdp', 'tp'), may hold values from -0.078125 to 0.078125
- cotangent: bfloat16 [4096, 2048], P(('fsdp', 'ctx')), may hold values from -6 to 6
Outputs:
- out: bfloat16 [4096, 2048], P(('fsdp', 'ctx'))
- d_tokens: bfloat16 [4096, 2048], P(('fsdp', 'ctx'))
- d_w_query: float32 [2048, 2048], P(('fsdp', 'ctx'), 'tp')
- d_w_key: float32 [2048, 2048], P(('fsdp', 'ctx'), 'tp')
- d_w_value: float32 [2048, 2048], P(('fsdp', 'ctx'), 'tp')
- d_w_beta: float32 [2048, 16], P(('fsdp', 'ctx'), 'tp')
- d_conv_taps: float32 [3, 4, 2048], P(None, None, 'tp')
- d_out_gain: float32 [128], replicated
- d_w_out: float32 [2048, 2048], P(('fsdp', 'ctx'), 'tp')
- d_attn_gain: float32 [2048], replicated
- d_ffn_gain: float32 [2048], replicated
- d_w_gate: float32 [2048, 5632], P(('fsdp', 'ctx'), 'tp')
- d_w_up: float32 [2048, 5632], P(('fsdp', 'ctx'), 'tp')
- d_w_down: float32 [2048, 5632], P(('fsdp', 'ctx'), 'tp')
Inputs may be any that keep to these rules, and one draw needn't show every extreme that they name: `seq_bounds`: row t holds e0 <= e1 < e2 for stream t, with e0 < 256 and 1664 <= e1 <= 1920; in every draw some stream has e2 = 2048 and some stream has e0 = 0.
All inputs are finite; a program needn't handle non-finite values.
Results may differ from a plain program's by a relative error of at most 0.023.
Values may be sent and summed in bfloat16 or wider, within the bound.
No kernel may reach another device: no remote copies, remote signals or barrier semaphores. Data moves between devices by JAX's collectives and lax.ppermute only.
A program may use at most 192 MiB of HBM per device.

v0:
```python
import math

import jax
import jax.numpy as jnp
from jax import lax
from jax.sharding import PartitionSpec as P

GROUP = 64


EPS = 1e-06
HIGH = lax.Precision.HIGHEST


def shifted(shard, axis, by):
    length = lax.axis_size(axis)
    pairs = [(i, i + by) for i in range(length) if 0 <= i + by < length]
    return lax.ppermute(shard, axis, pairs)


def inner(form, left_side, right_side):
    return jnp.einsum(
        form, left_side, right_side, precision=HIGH, preferred_element_type=jnp.float32
    )


def contract_rows(left_side, right_side):
    return lax.dot_general(
        left_side, right_side, (((0,), (0,)), ((), ())), preferred_element_type=jnp.float32
    )


def contract_cols(left_side, right_side):
    return lax.dot_general(
        left_side, right_side, (((1,), (1,)), ((), ())), preferred_element_type=jnp.float32
    )


def unit_rows(values):
    return values * lax.rsqrt(jnp.sum(values * values, axis=-1, keepdims=True) + EPS)


def rms_norm(values, gain):
    return values * lax.rsqrt(jnp.mean(values * values, axis=-1, keepdims=True) + EPS) * gain


def norm_backward(grad_normed, values, gain):
    scale = lax.rsqrt(jnp.mean(values * values, axis=-1, keepdims=True) + EPS)
    normal = values * scale
    grad_hat = grad_normed * gain
    grad_values = scale * (grad_hat - normal * jnp.mean(grad_hat * normal, axis=-1, keepdims=True))
    return (grad_values, jnp.sum(grad_normed * normal, axis=0))


def segment_ids(places, bounds):
    ids = jnp.zeros(places.shape, jnp.int32)
    for index in range(3):
        ids = ids + (places >= bounds[index]).astype(jnp.int32)
    return jnp.where(places < 0, jnp.int32(-1), ids)


def block_masks(seg_block, prev_id):
    same = (seg_block[:, None] == seg_block[None, :]).astype(jnp.float32)
    carry_in = (seg_block == prev_id).astype(jnp.float32)
    tail = (seg_block == seg_block[-1]).astype(jnp.float32)
    whole = (seg_block[-1] == prev_id).astype(jnp.float32)
    return (same, carry_in, tail, whole)


def group_parts(keys_unit, values, strength, same):
    scaled = keys_unit * strength[..., None]
    gram = inner("hid,hjd->hij", scaled, keys_unit) * same[None]
    system = jnp.eye(keys_unit.shape[1], dtype=jnp.float32) + jnp.tril(gram, -1)
    right_hand = jnp.concatenate([scaled, values * strength[..., None]], axis=2)
    solved = jax.scipy.linalg.solve_triangular(system, right_hand, lower=True, unit_diagonal=True)
    return (solved[..., : keys_unit.shape[2]], solved[..., keys_unit.shape[2] :])


def group_advance(state, block):
    queries, keys_unit, values, strength, seg_block, prev_id = block
    same, carry_in, tail, whole = block_masks(seg_block, prev_id)
    erase, write = group_parts(keys_unit, values, strength, same)
    fresh = write - carry_in[None, :, None] * inner("hcd,hde->hce", erase, state)
    scores = jnp.tril(inner("hid,hjd->hij", queries, keys_unit) * same[None])
    output = carry_in[None, :, None] * inner("hcd,hde->hce", queries, state) + inner(
        "hij,hje->hie", scores, fresh
    )
    return (whole * state + inner("hcd,hce->hde", keys_unit, tail[None, :, None] * fresh), output)


def transition_step(carry, block):
    keys_unit, values, strength, seg_block, prev_id = block
    same, carry_in, tail, whole = block_masks(seg_block, prev_id)
    erase, write = group_parts(keys_unit, values, strength, same)
    extended = jnp.concatenate([jnp.zeros_like(write), write], axis=2)
    fresh = extended - carry_in[None, :, None] * inner("hcd,hde->hce", erase, carry)
    return (whole * carry + inner("hcd,hce->hde", keys_unit, tail[None, :, None] * fresh), None)


def to_blocks(values, block_rows):
    count = values.shape[0] // block_rows
    if values.ndim == 3:
        return values.reshape(count, block_rows, values.shape[1], values.shape[2]).transpose(
            0, 2, 1, 3
        )
    return values.reshape(count, block_rows, values.shape[1]).transpose(0, 2, 1)


def shards(
    tokens,
    seq_bounds,
    w_query,
    w_key,
    w_value,
    w_beta,
    conv_taps,
    out_gain,
    w_out,
    attn_gain,
    ffn_gain,
    w_gate,
    w_up,
    w_down,
    cotangent,
):
    row_count = tokens.shape[0]
    heads_here = w_beta.shape[1]
    head_dim = out_gain.shape[0]
    tap_count = conv_taps.shape[1]
    channels = w_query.shape[1]
    bounds = seq_bounds[0]
    first_place = lax.axis_index("ctx") * row_count
    places = first_place + jnp.arange(row_count, dtype=jnp.int32)
    mask = (places < bounds[2]).astype(jnp.float32)
    seg_rows = segment_ids(places, bounds)
    ext_seg = segment_ids(
        first_place - (tap_count - 1) + jnp.arange(row_count + tap_count - 1, dtype=jnp.int32),
        bounds,
    )
    tap_same = [
        (
            ext_seg[tap_count - 1 - tap_index : tap_count - 1 - tap_index + row_count] == seg_rows
        ).astype(jnp.float32)[:, None]
        for tap_index in range(tap_count)
    ]
    block_count = row_count // GROUP
    seg_blocks = seg_rows.reshape(block_count, GROUP)
    prev_ids = segment_ids(
        first_place + jnp.arange(block_count, dtype=jnp.int32) * GROUP - 1, bounds
    )
    inputs = tokens.astype(jnp.float32)
    query_full, key_full, value_full, beta_full, out_full = (
        lax.all_gather(w_query, "fsdp", axis=0, tiled=True),
        lax.all_gather(w_key, "fsdp", axis=0, tiled=True),
        lax.all_gather(w_value, "fsdp", axis=0, tiled=True),
        lax.all_gather(w_beta, "fsdp", axis=0, tiled=True),
        lax.all_gather(w_out, "fsdp", axis=0, tiled=True),
    )
    proj_weight = jnp.concatenate([query_full, key_full, value_full], axis=1)
    normed = rms_norm(inputs, attn_gain).astype(jnp.bfloat16)
    projected = jnp.dot(normed, proj_weight, preferred_element_type=jnp.float32)
    logits = jnp.dot(normed, beta_full, preferred_element_type=jnp.float32)
    rim_in = shifted(normed[row_count - tap_count + 1 :], "ctx", 1)
    rim_proj = jnp.dot(rim_in, proj_weight, preferred_element_type=jnp.float32)
    extended = jnp.concatenate([rim_proj, projected], axis=0)

    def prepare(extended_rows, kernel_taps, logit_rows):
        kernel = jnp.concatenate([kernel_taps[0], kernel_taps[1], kernel_taps[2]], axis=1)
        mixed = jnp.zeros((row_count, kernel.shape[1]), jnp.float32)
        for tap_index in range(tap_count):
            offset = tap_count - 1 - tap_index
            mixed = (
                mixed
                + kernel[tap_index]
                * extended_rows[offset : offset + row_count]
                * tap_same[tap_index]
            )
        mixed = jax.nn.silu(mixed)
        width = kernel.shape[1] // 3
        queries = unit_rows(mixed[:, :width].reshape(row_count, heads_here, head_dim)) * (
            1.0 / math.sqrt(head_dim)
        )
        keys_unit = unit_rows(mixed[:, width : 2 * width].reshape(row_count, heads_here, head_dim))
        values = mixed[:, 2 * width :].reshape(row_count, heads_here, head_dim)
        strength = jax.nn.sigmoid(logit_rows) * mask[:, None]
        return (queries, keys_unit, values, strength)

    def core(extended_rows, kernel_taps, logit_rows, head_gain, state_in):
        queries, keys_unit, values, strength = prepare(extended_rows, kernel_taps, logit_rows)
        blocks = (
            to_blocks(queries, GROUP),
            to_blocks(keys_unit, GROUP),
            to_blocks(values, GROUP),
            to_blocks(strength, GROUP),
            seg_blocks,
            prev_ids,
        )
        state_out, outputs = lax.scan(group_advance, state_in, blocks)
        heads_out = outputs.transpose(0, 2, 1, 3).reshape(row_count, heads_here, head_dim)
        return (rms_norm(heads_out, head_gain).reshape(row_count, heads_here * head_dim), state_out)

    queries, keys_unit, values, strength = prepare(extended, conv_taps, logits)
    identity = jnp.broadcast_to(
        jnp.eye(head_dim, dtype=jnp.float32), (heads_here, head_dim, head_dim)
    )
    zero_state = jnp.zeros((heads_here, head_dim, head_dim), jnp.float32)
    start_carry = jnp.concatenate([identity, zero_state], axis=2)
    carry, unused = lax.scan(
        transition_step,
        start_carry,
        (
            to_blocks(keys_unit, GROUP),
            to_blocks(values, GROUP),
            to_blocks(strength, GROUP),
            seg_blocks,
            prev_ids,
        ),
    )
    state_map = carry[..., :head_dim]
    state_add = carry[..., head_dim:]

    def pass_forward(step_index, state):
        return shifted(
            (inner("hij,hjk->hik", state_map, state) + state_add).astype(jnp.bfloat16), "ctx", 1
        ).astype(jnp.float32)

    state_in = lax.fori_loop(0, lax.axis_size("ctx") - 1, pass_forward, zero_state)
    (heads_normed, state_out), pullback = jax.vjp(
        core, extended, conv_taps, logits, out_gain, state_in
    )
    heads_low = heads_normed.astype(jnp.bfloat16)
    partial_att = contract_cols(heads_low, out_full)
    gate_full, up_full, down_full = (
        lax.all_gather(w_gate, "fsdp", axis=0, tiled=True),
        lax.all_gather(w_up, "fsdp", axis=0, tiled=True),
        lax.all_gather(w_down, "fsdp", axis=0, tiled=True),
    )
    hidden = inputs + lax.psum(partial_att.astype(jnp.bfloat16), "tp").astype(jnp.float32)
    normed_two = rms_norm(hidden, ffn_gain).astype(jnp.bfloat16)
    gate = jnp.dot(normed_two, gate_full, preferred_element_type=jnp.float32)
    up_proj = jnp.dot(normed_two, up_full, preferred_element_type=jnp.float32)
    sigma = jax.nn.sigmoid(gate)
    act = (gate * sigma * up_proj).astype(jnp.bfloat16)
    partial_down = contract_cols(act, down_full)
    out_rows = (
        hidden + lax.psum(partial_down.astype(jnp.bfloat16), "tp").astype(jnp.float32)
    ).astype(jnp.bfloat16)
    grad_out = cotangent.astype(jnp.float32) * mask[:, None]
    grad_low = grad_out.astype(jnp.bfloat16)
    d_w_down = contract_rows(grad_low, act)
    grad_act = jnp.dot(grad_low, down_full, preferred_element_type=jnp.float32)
    grad_gate = (grad_act * up_proj * sigma * (1.0 + gate * (1.0 - sigma))).astype(jnp.bfloat16)
    grad_up = (grad_act * gate * sigma).astype(jnp.bfloat16)
    d_w_gate = contract_rows(normed_two, grad_gate)
    d_w_up = contract_rows(normed_two, grad_up)
    partial_back = contract_cols(grad_gate, gate_full) + contract_cols(grad_up, up_full)
    grad_normed_two = lax.psum(partial_back.astype(jnp.bfloat16), "tp").astype(jnp.float32)
    grad_from_norm, d_ffn_gain = norm_backward(grad_normed_two, hidden, ffn_gain)
    grad_hidden = grad_out + grad_from_norm
    grad_att = grad_hidden.astype(jnp.bfloat16)
    d_w_out = contract_rows(grad_att, heads_low)
    grad_heads = jnp.dot(grad_att, out_full, preferred_element_type=jnp.float32)
    direct_terms = pullback((grad_heads, zero_state))[4]
    map_back = jnp.swapaxes(state_map, 1, 2)

    def pass_backward(step_index, grad_state):
        return shifted(
            (inner("hij,hjk->hik", map_back, grad_state) + direct_terms).astype(jnp.bfloat16),
            "ctx",
            -1,
        ).astype(jnp.float32)

    grad_state_out = lax.fori_loop(0, lax.axis_size("ctx") - 1, pass_backward, zero_state)
    grad_extended, d_conv_local, grad_logit_rows, d_head_gain, unused_state = pullback(
        (grad_heads, grad_state_out)
    )
    returned = shifted(grad_extended[: tap_count - 1], "ctx", -1)
    grad_proj = grad_extended[tap_count - 1 :] + jnp.concatenate(
        [jnp.zeros((row_count - tap_count + 1, returned.shape[1]), jnp.float32), returned], axis=0
    )
    grad_proj_low = grad_proj.astype(jnp.bfloat16)
    grad_logit_low = grad_logit_rows.astype(jnp.bfloat16)
    d_w_proj = contract_rows(normed, grad_proj_low)
    d_w_beta = contract_rows(normed, grad_logit_low)
    grad_normed_part = contract_cols(grad_proj_low, proj_weight) + contract_cols(
        grad_logit_low, beta_full
    )
    grad_normed, d_head_gain_sum = (
        lax.psum(grad_normed_part.astype(jnp.bfloat16), "tp").astype(jnp.float32),
        lax.psum(d_head_gain.astype(jnp.bfloat16), "tp").astype(jnp.float32),
    )
    grad_input_norm, d_attn_gain = norm_backward(grad_normed, inputs, attn_gain)
    d_tokens = (grad_hidden + grad_input_norm).astype(jnp.bfloat16)
    small_parts = (
        lax.psum(d_conv_local.astype(jnp.bfloat16), ("fsdp", "ctx")).astype(jnp.float32),
        lax.psum(d_head_gain_sum.astype(jnp.bfloat16), ("fsdp", "ctx")).astype(jnp.float32),
        lax.psum(d_attn_gain.astype(jnp.bfloat16), ("fsdp", "ctx")).astype(jnp.float32),
        lax.psum(d_ffn_gain.astype(jnp.bfloat16), ("fsdp", "ctx")).astype(jnp.float32),
    )
    d_conv = small_parts[0]
    grad_parts = (
        lax.psum_scatter(
            d_w_proj[:, :channels].astype(jnp.bfloat16),
            ("fsdp", "ctx"),
            scatter_dimension=0,
            tiled=True,
        ).astype(jnp.float32),
        lax.psum_scatter(
            d_w_proj[:, channels : 2 * channels].astype(jnp.bfloat16),
            ("fsdp", "ctx"),
            scatter_dimension=0,
            tiled=True,
        ).astype(jnp.float32),
        lax.psum_scatter(
            d_w_proj[:, 2 * channels :].astype(jnp.bfloat16),
            ("fsdp", "ctx"),
            scatter_dimension=0,
            tiled=True,
        ).astype(jnp.float32),
        lax.psum_scatter(
            d_w_beta.astype(jnp.bfloat16), ("fsdp", "ctx"), scatter_dimension=0, tiled=True
        ).astype(jnp.float32),
        lax.psum_scatter(
            d_w_out.astype(jnp.bfloat16), ("fsdp", "ctx"), scatter_dimension=0, tiled=True
        ).astype(jnp.float32),
        lax.psum_scatter(
            d_w_gate.astype(jnp.bfloat16), ("fsdp", "ctx"), scatter_dimension=0, tiled=True
        ).astype(jnp.float32),
        lax.psum_scatter(
            d_w_up.astype(jnp.bfloat16), ("fsdp", "ctx"), scatter_dimension=0, tiled=True
        ).astype(jnp.float32),
        lax.psum_scatter(
            d_w_down.astype(jnp.bfloat16), ("fsdp", "ctx"), scatter_dimension=0, tiled=True
        ).astype(jnp.float32),
    )
    return (
        out_rows,
        d_tokens,
        grad_parts[0],
        grad_parts[1],
        grad_parts[2],
        grad_parts[3],
        d_conv,
        small_parts[1],
        grad_parts[4],
        small_parts[2],
        small_parts[3],
        grad_parts[5],
        grad_parts[6],
        grad_parts[7],
    )


def solution(mesh):
    in_specs = (
        P(("fsdp", "ctx"), None),
        P("fsdp", None),
        P("fsdp", "tp"),
        P("fsdp", "tp"),
        P("fsdp", "tp"),
        P("fsdp", "tp"),
        P(None, None, "tp"),
        P(),
        P("fsdp", "tp"),
        P(),
        P(),
        P("fsdp", "tp"),
        P("fsdp", "tp"),
        P("fsdp", "tp"),
        P(("fsdp", "ctx"), None),
    )
    out_specs = (
        P(("fsdp", "ctx"), None),
        P(("fsdp", "ctx"), None),
        P(("fsdp", "ctx"), "tp"),
        P(("fsdp", "ctx"), "tp"),
        P(("fsdp", "ctx"), "tp"),
        P(("fsdp", "ctx"), "tp"),
        P(None, None, "tp"),
        P(),
        P(("fsdp", "ctx"), "tp"),
        P(),
        P(),
        P(("fsdp", "ctx"), "tp"),
        P(("fsdp", "ctx"), "tp"),
        P(("fsdp", "ctx"), "tp"),
    )
    return jax.shard_map(shards, mesh=mesh, in_specs=in_specs, out_specs=out_specs, check_vma=False)
```

profile of v0, /device:TPU:16, one launch (start us, length us, event | category | flops | bytes accessed | tf_op | source)
XLA Modules:
  0.0 2320.6 jit_solution(16972620358737090705)
XLA Ops:
  75.5 302.3 %while.119 = (s32[]{:T(128)}, f32[4,128,256]{2,1,0:T(8,128)}, s32[8,64]{1,0:T(8,128)}, s32[8]{0:T(128)}, f32[8,4,64,128]{3,2,1,0:T(8,128)S(1)}, /*index=5*/f32[8...) while((s32[]{:T(128)}, f32[4,128,256]{2,1,0:T(8,128)}, s32[8,64]{1,0:T(8,128)}, s32[8]{0:T(128)}, ...), condition=%wide.region_3.5_spmd, body=%wide.region_2.4_spmd.sunk | while | flops 277524800 | bytes 4361147 | solution.py:208
  82.5 21.0 custom-call.40
  120.3 21.0 custom-call.40
  271.4 21.0 custom-call.40
  396.6 28.7 %while.122 = (s32[]{:T(128)}, f32[4,128,128]{2,1,0:T(8,128)S(1)}, f32[4,128,128]{2,1,0:T(8,128)}, f32[4,128,128]{2,1,0:T(8,128)}, s32[]{:T(128)}, /*index=5*/s32[]{:T(128)}) while((s32[]{:T(128)}, f32[4,128,128]{2,1,0:T(8,128)S(1)}, f32[4,128,128]{2,1,0:T(8,128)}, f32[4,128,128]{2,1,0:T(8,128)}, s32[]{:T(128)}, ...), condition=%wide.region_5.7_spmd.clone, body=%wide.region_4.6_spmd.clone.sunk | while | flops 100925440 | bytes 1835127 | solution.py:227
  430.9 423.7 %while.120 = (s32[]{:T(128)}, f32[4,128,128]{2,1,0:T(8,128)S(1)}, f32[8,4,64,128]{3,2,1,0:T(8,128)}, f32[8,4,64,1]{2,1,3,0:T(4,128)}, f32[8,4,64,128]{3,2,1,0:T(...) while((s32[]{:T(128)}, f32[4,128,128]{2,1,0:T(8,128)S(1)}, ...), condition=%wide.region_8.10_spmd.clone, body=%wide.region_7.9_spmd.clone.sunk | while | flops 277467712 | bytes 8831963 | solution.py:198
  655.4 21.0 custom-call.41
  814.1 21.0 custom-call.41
  867.7 68.4 %all-reduce.25.cloned.1.call-done = bf16[512,2048]{1,0:T(8,128)(2,1)} async-done(((bf16[512,2048]{1,0:T(8,128)(2,1)}), bf16[512,2048]{1,0:T(8,128)(2,1)}) %all-reduce.25.cloned.1.call-update) | async-done | bytes 2097168 | tf_op jit(solution)/shard_map/psum | solution.py:238
  1022.2 61.7 %all-reduce.27.cloned.1.call-done = bf16[512,2048]{1,0:T(8,128)(2,1)} async-done(((bf16[512,2048]{1,0:T(8,128)(2,1)}), bf16[512,2048]{1,0:T(8,128)(2,1)}) %all-reduce.27.cloned.1.call-update) | async-done | bytes 2097168 | tf_op jit(solution)/shard_map/psum | solution.py:257
  1108.6 66.2 %while.123 = (s32[]{:T(128)}, f32[4,128,128]{2,1,0:T(8,128)}, f32[8]{0:T(128)S(1)}, f32[8,4,64,128]{3,2,1,0:T(8,128)}, f32[8,1,64,1]{2,3,1,0:T(1,128)}, /*index=...) while((s32[]{:T(128)}, f32[4,128,128]{2,1,0:T(8,128)}, ...), condition=%wide.region_17.19_spmd.clone, body=%wide.region_16.18_spmd.clone.sunk | while | flops 176652288 | bytes 2626995 | solution.py:198
  1174.8 28.3 %while.124 = (s32[]{:T(128)}, f32[4,128,128]{2,1,0:T(8,128)S(1)}, f32[4,128,128]{2,1,0:T(8,128)}, f32[4,128,128]{2,1,0:T(8,128)}, s32[]{:T(128)}, /*index=5*/s32[]{:T(128)}) while((s32[]{:T(128)}, f32[4,128,128]{2,1,0:T(8,128)S(1)}, f32[4,128,128]{2,1,0:T(8,128)}, f32[4,128,128]{2,1,0:T(8,128)}, s32[]{:T(128)}, ...), condition=%wide.region_19.21_spmd.clone, body=%wide.region_18.20_spmd.clone.sunk | while | flops 100925440 | bytes 1835127 | solution.py:273
  1207.0 393.1 %while.121 = (s32[]{:T(128)}, f32[4,128,128]{2,1,0:T(8,128)S(1)}, f32[8,4,64,128]{3,2,1,0:T(8,128)}, f32[8,4,64,128]{3,2,1,0:T(8,128)}, f32[8,4,64,128]{3,2,1,0:...) while((s32[]{:T(128)}, f32[4,128,128]{2,1,0:T(8,128)S(1)}, ...), condition=%wide.region_23.25_spmd.clone.clone, body=%wide.region_20.24_spmd.clone.clone.sunk | while | flops 567324480 | bytes 9443893 | solution.py:198
  1215.6 21.0 custom-call.42
  1264.7 21.0 custom-call.42
  1461.1 21.0 custom-call.42
  1510.2 21.0 custom-call.42
  1689.3 106.7 %all-reduce.29.cloned.1.call-done = (bf16[512,2048]{1,0:T(8,128)(2,1)}, bf16[512,2048]{1,0:T(8,128)(2,1)}) async-done(((bf16[512,2048]{1,0:T(8,128)(2,1)}, bf16[512,2048]{1,0:T(8,128)(2,1)}), (bf16[512,2048]{1,0:T(8,128)(2,1)}, bf16[512,2048]{1,0:T(8,128)(2,1)})) %all-reduce.29.cloned.1.call-update) | async-done | bytes 4194320 | tf_op jit(solution)/shard_map/psum | solution.py:246
  1799.0 30.2 %all-reduce.19 = (bf16[3,4,512]{2,1,0:T(4,128)(2,1)S(1)}, bf16[128]{0:T(256)(128)(2,1)S(1)}, bf16[2048]{0:T(1024)(128)(2,1)S(1)}, bf16[2048]{0:T(1024)(128)(2,1)S(1)}) all-reduce(bf16[3,4,512]{2,1,0:T(4,128)(2,1)S(1)} %add_convert_fusion.3, bf16[128]{0:T(256)(128)(2,1)S(1)} %psum.68, ...), channel_id=1, replica_groups=mesh['fsdp'=2,'ctx'=4,'tp'=4] {'fsdp','ctx'}, use_global_device_ids=true, to_apply=%region_36.38 | all-reduce | flops 10368 | bytes 41472 | tf_op jit(solution)/shard_map/psum | solution.py:295
  1849.5 48.6 %reduce-scatter.13.cloned.1.call-done = bf16[256,512]{1,0:T(8,128)(2,1)} async-done(((bf16[2048,512]{1,0:T(8,128)(2,1)}), bf16[256,512]{1,0:T(8,128)(2,1)}) %reduce-scatter.13.cloned.1.call-update) | async-done | bytes 262160 | tf_op jit(solution)/shard_map/reduce_scatter | solution.py:308
  1899.9 49.2 %reduce-scatter.15.cloned.1.call-done = bf16[256,512]{1,0:T(8,128)(2,1)} async-done(((bf16[2048,512]{1,0:T(8,128)(2,1)}), bf16[256,512]{1,0:T(8,128)(2,1)}) %reduce-scatter.15.cloned.1.call-update) | async-done | bytes 262160 | tf_op jit(solution)/shard_map/reduce_scatter | solution.py:314
  1957.6 112.2 %reduce-scatter.19.cloned.1.call-done = bf16[256,1408]{1,0:T(8,128)(2,1)} async-done(((bf16[2048,1408]{1,0:T(8,128)(2,1)}), bf16[256,1408]{1,0:T(8,128)(2,1)}) %reduce-scatter.19.cloned.1.call-update) | async-done | bytes 720912 | tf_op jit(solution)/shard_map/reduce_scatter | solution.py:326
  2072.1 118.4 %reduce-scatter.21.cloned.1.call-done = bf16[256,1408]{1,0:T(8,128)(2,1)} async-done(((bf16[2048,1408]{1,0:T(8,128)(2,1)}), bf16[256,1408]{1,0:T(8,128)(2,1)}) %reduce-scatter.21.cloned.1.call-update) | async-done | bytes 720912 | tf_op jit(solution)/shard_map/reduce_scatter | solution.py:329
  2192.8 118.4 %reduce-scatter.23.cloned.1.call-done = bf16[256,1408]{1,0:T(8,128)(2,1)} async-done(((bf16[2048,1408]{1,0:T(8,128)(2,1)}), bf16[256,1408]{1,0:T(8,128)(2,1)}) %reduce-scatter.23.cloned.1.call-update) | async-done | bytes 720912 | tf_op jit(solution)/shard_map/reduce_scatter | solution.py:332
  (1138 shorter events, 1378.3 us)
Async XLA Ops:
  7.2 25.8 %all-gather.8.cloned.1.call-start = ((), (), s32[]{:S(2)}) async-start(), calls=%async_computation.8 | async-start | bytes 3145728 | tf_op jit(solution)/shard_map/all_gather | solution.py:153
  7.9 28.2 %all-gather.10.cloned.1.call-start = ((), (), s32[]{:S(2)}) async-start(), calls=%async_computation.9 | async-start | bytes 3145728 | tf_op jit(solution)/shard_map/all_gather | solution.py:154
  8.7 39.5 %all-gather.12.cloned.1.call-start = ((), (), s32[]{:S(2)}) async-start(), calls=%async_computation.10 | async-start | bytes 3145728 | tf_op jit(solution)/shard_map/all_gather | solution.py:155
  9.4 851.5 %all-gather.14.cloned.1.call-start = ((), (), s32[]{:S(2)}) async-start(), calls=%async_computation.11 | async-start | bytes 3145728 | tf_op jit(solution)/shard_map/all_gather | solution.py:157
  11.9 45.5 %collective-permute-start.2 = (bf16[3,2048]{1,0:T(4,128)(2,1)S(1)}, bf16[3,2048]{1,0:T(4,128)(2,1)S(1)}, u32[]{:S(2)}, u32[]{:S(2)}) collective-permute-start(bf16[3,2048]{1,0:T(4,128)(2,1)S(1)} %slice.197), channel_id=1, source_target_pairs={{0,4},{4,8},{8,12},{1,5},{5,9},{9,13},{2,6},{6,10},{10,14},{3,7},{... | collective-permute-start | bytes 36872 | tf_op jit(solution)/shard_map/ppermute | solution.py:18
  15.4 920.6 %all-reduce.25.cloned.1.call-start = ((), (), s32[]{:S(2)}) async-start(), calls=%async_computation.12 | async-start | bytes 4194304 | tf_op jit(solution)/shard_map/psum | solution.py:238
  398.0 7.7 collective-permute-start
  408.1 7.0 collective-permute-start
  417.4 7.0 collective-permute-start
  865.3 88.5 %all-gather.16.cloned.1.call-start = ((), (), s32[]{:S(2)}) async-start(), calls=%async_computation.13 | async-start | bytes 8650752 | tf_op jit(solution)/shard_map/all_gather | solution.py:234
  865.9 106.7 %all-gather.18.cloned.1.call-start = ((), (), s32[]{:S(2)}) async-start(), calls=%async_computation.14 | async-start | bytes 8650752 | tf_op jit(solution)/shard_map/all_gather | solution.py:235
  866.7 124.7 %all-gather.20.cloned.1.call-start = ((), (), s32[]{:S(2)}) async-start(), calls=%async_computation.15 | async-start | bytes 8650752 | tf_op jit(solution)/shard_map/all_gather | solution.py:236
  867.4 216.4 %all-reduce.27.cloned.1.call-start = ((), (), s32[]{:S(2)}) async-start(), calls=%async_computation.16 | async-start | bytes 4194304 | tf_op jit(solution)/shard_map/psum | solution.py:257
  1013.2 672.8 %reduce-scatter.25.cloned.1.call-start = ((), (), s32[]{:S(2)}) async-start(), calls=%async_computation.24 | async-start | bytes 589824
  1176.2 7.2 collective-permute-start.1
  1185.9 7.0 collective-permute-start.1
  1606.2 81.3 %reduce-scatter.17.cloned.1.call-start = ((), (), s32[]{:S(2)}) async-start(), calls=%async_computation.20 | async-start | bytes 2359296 | tf_op jit(solution)/shard_map/reduce_scatter | solution.py:323
  1616.4 179.7 %all-reduce.29.cloned.1.call-start = ((), (), s32[]{:S(2)}) async-start(), calls=%async_computation.25 | async-start | bytes 8388608 | tf_op jit(solution)/shard_map/psum | solution.py:246
  1641.5 206.2 %reduce-scatter.11.cloned.1.call-start = ((), (), s32[]{:S(2)}) async-start(), calls=%async_computation.17 | async-start | bytes 2359296 | tf_op jit(solution)/shard_map/reduce_scatter | solution.py:302
  1650.7 247.4 %reduce-scatter.13.cloned.1.call-start = ((), (), s32[]{:S(2)}) async-start(), calls=%async_computation.18 | async-start | bytes 2359296 | tf_op jit(solution)/shard_map/reduce_scatter | solution.py:308
  1651.2 297.8 %reduce-scatter.15.cloned.1.call-start = ((), (), s32[]{:S(2)}) async-start(), calls=%async_computation.19 | async-start | bytes 2359296 | tf_op jit(solution)/shard_map/reduce_scatter | solution.py:314
  1651.8 417.9 %reduce-scatter.19.cloned.1.call-start = ((), (), s32[]{:S(2)}) async-start(), calls=%async_computation.21 | async-start | bytes 6488064 | tf_op jit(solution)/shard_map/reduce_scatter | solution.py:326
  1659.9 530.5 %reduce-scatter.21.cloned.1.call-start = ((), (), s32[]{:S(2)}) async-start(), calls=%async_computation.22 | async-start | bytes 6488064 | tf_op jit(solution)/shard_map/reduce_scatter | solution.py:329
  1667.9 643.2 %reduce-scatter.23.cloned.1.call-start = ((), (), s32[]{:S(2)}) async-start(), calls=%async_computation.23 | async-start | bytes 6488064 | tf_op jit(solution)/shard_map/reduce_scatter | solution.py:332
  (159 other events, 1331.8 us)
Sparse Core Ops, SparseCore 0:
  9.6 11.9 all-gather.7
  23.1 11.7 all-gather.9
  36.4 11.7 all-gather.11
  49.6 11.7 all-gather.13
  865.5 70.5 all-reduce.24
  937.5 16.2 all-gather.15
  955.4 17.1 all-gather.17
  974.2 17.1 all-gather.19
  1013.3 70.5 all-reduce.26
  1606.3 30.5 reduce-scatter.24
  1639.3 48.1 reduce-scatter.16
  1691.8 104.1 all-reduce.28
  1798.4 49.2 reduce-scatter.10
  1849.8 48.2 reduce-scatter.12
  1900.8 48.2 reduce-scatter.14
  1951.2 118.4 reduce-scatter.18
  2071.9 118.4 reduce-scatter.20
  2192.6 118.4 reduce-scatter.22
where the time goes:
time: 2340 us; the launch traced here: 2320 us
  waiting for transfers between devices  773 us (33%)
  other arithmetic  752 us (32%)
  matrix products  470 us (20%)
  local copies, waits for them, and re-layouts  220 us (9%)
  blocking collectives  40.9 us (2%)
  starting transfers between devices  25.5 us (1%)
    another operation x104, other arithmetic, group_parts(): jax.scipy.linalg.solve_triangular(system, right_hand, lower=True, unit_di...  525 us
    dot_general x206, matrix products, inner(): jnp.einsum(form, left_side, right_side, precision=HIGH, preferred_element...  301 us
    reduce_scatter x1, waiting for transfers between devices, shards(): lax.psum_scatter(d_w_down.astype(jnp.bfloat16), ('fsdp', 'ctx'), scatter_...  118 us
    reduce_scatter x1, waiting for transfers between devices, shards(): lax.psum_scatter(d_w_up.astype(jnp.bfloat16), ('fsdp', 'ctx'), scatter_di...  118 us
    reduce_scatter x1, waiting for transfers between devices, shards(): lax.psum_scatter(d_w_gate.astype(jnp.bfloat16), ('fsdp', 'ctx'), scatter_...  112 us
    psum x1, waiting for transfers between devices, shards(): lax.psum(partial_down.astype(jnp.bfloat16), 'tp').astype(jnp.float32)  107 us
    psum x1, waiting for transfers between devices, shards(): lax.psum(partial_att.astype(jnp.bfloat16), 'tp').astype(jnp.float32)  68.4 us
    dynamic_update_slice x48, other arithmetic, core(): state_out, outputs = lax.scan(group_advance, state_in, blocks)  65.5 us
  transfers between devices with their start and end apart: 26, of which 19 were waited for; matrix products, arithmetic and copies ran while one was open for 38% of the time, Pallas kernels for 0%

commit v1 on v0

v1 whole, which is shorter than its diff:
```python
import functools
import math

import jax
import jax.numpy as jnp
from jax import lax
from jax.experimental import pallas as pl
from jax.experimental.pallas import tpu as pltpu
from jax.sharding import PartitionSpec as P

EPS = 1e-06
HIGH = lax.Precision.HIGHEST
F32 = jnp.float32
BF16 = jnp.bfloat16
CHUNK = 128
RIM = 16
TAPS = 4
VMEM = pltpu.VMEM
WHOLE = pl.BlockSpec(memory_space=pltpu.VMEM)
SCALARS = pl.BlockSpec(memory_space=pltpu.SMEM)


def dot_nn(left, right, precision=None):
    return lax.dot_general(
        left, right, (((1,), (0,)), ((), ())), precision=precision, preferred_element_type=F32
    )


def dot_nt(left, right, precision=None):
    return lax.dot_general(
        left, right, (((1,), (1,)), ((), ())), precision=precision, preferred_element_type=F32
    )


def dot_tn(left, right, precision=None):
    return lax.dot_general(
        left, right, (((0,), (0,)), ((), ())), precision=precision, preferred_element_type=F32
    )


def call(kernel, out_shape, operands, flops=0, scratch=(), grid=None, in_specs=None, out_specs=None):
    size = sum(math.prod(x.shape) * x.dtype.itemsize for x in operands)
    outs = out_shape if isinstance(out_shape, (list, tuple)) else [out_shape]
    size += sum(math.prod(x.shape) * x.dtype.itemsize for x in outs)
    extra = {} if grid is None else {"grid": grid}
    return pl.pallas_call(
        kernel,
        out_shape=out_shape,
        in_specs=in_specs or [SCALARS] + [WHOLE] * (len(operands) - 1),
        out_specs=out_specs or (type(out_shape)([WHOLE] * len(outs)) if isinstance(out_shape, (list, tuple)) else WHOLE),
        scratch_shapes=list(scratch),
        cost_estimate=pl.CostEstimate(flops=flops, bytes_accessed=size, transcendentals=0),
        compiler_params=pltpu.CompilerParams(vmem_limit_bytes=58 << 20),
        **extra,
    )(*operands)


def shape(*dims, dtype=F32):
    return jax.ShapeDtypeStruct(dims, dtype)


def seg_of(places, meta):
    ids = (
        (places >= meta[0]).astype(jnp.int32)
        + (places >= meta[1]).astype(jnp.int32)
        + (places >= meta[2]).astype(jnp.int32)
    )
    return jnp.where(places < 0, -1, ids)


def row_of(meta, slot, rows):
    return pl.ds(pl.multiple_of(meta[6 + slot], rows), rows)


def halves(meta, half):
    return (
        pl.ds(pl.multiple_of(meta[4], half), half),
        pl.ds(pl.multiple_of(meta[5], half), half),
    )


def project_kernel(meta, tok, rim, gain, wq, wk, wv, wb, xq, xk, xv, xb, normed, proj, logits, ext):
    rows, width = tok.shape
    for source, at, count in ((rim, 0, RIM), (tok, RIM, rows)):
        values = source[...].astype(F32)
        scale = lax.rsqrt(jnp.mean(values * values, axis=-1, keepdims=True) + EPS)
        ext[pl.ds(at, count), :] = (values * scale * gain[...]).astype(BF16)
    normed[...] = ext[pl.ds(RIM, rows), :]
    own, oth = halves(meta, width // 2)
    left, right = ext[:, own], ext[:, oth]
    chan = wq.shape[1]
    for at, (a, b) in enumerate(((wq, xq), (wk, xk), (wv, xv))):
        proj[:, at * chan : (at + 1) * chan] = dot_nn(left, a[...]) + dot_nn(right, b[...])
    logits[...] = dot_nn(left[RIM:], wb[...]) + dot_nn(right[RIM:], xb[...])


def conv_rows(ext, taps, rows, sames):
    mixed = None
    for j in range(TAPS):
        term = taps[j : j + 1, :] * ext[RIM - j : RIM - j + rows, :] * sames[j]
        mixed = term if mixed is None else mixed + term
    return mixed


def tap_masks(meta, rows):
    places = meta[3] + lax.broadcasted_iota(jnp.int32, (rows, 1), 0)
    seg = seg_of(places, meta)
    return places, [(seg_of(places - j, meta) == seg).astype(F32) for j in range(TAPS)]


def pick_column(values, head):
    lane = lax.broadcasted_iota(jnp.int32, values.shape, 1)
    return jnp.sum(jnp.where(lane == head, values, 0.0), axis=1, keepdims=True)


def chunk_masks(meta, at):
    first = meta[3] + at * CHUNK
    row = lax.broadcasted_iota(jnp.int32, (CHUNK, CHUNK), 0)
    col = lax.broadcasted_iota(jnp.int32, (CHUNK, CHUNK), 1)
    seg_col = seg_of(first + lax.broadcasted_iota(jnp.int32, (CHUNK, 1), 0), meta)
    seg_row = seg_of(first + lax.broadcasted_iota(jnp.int32, (1, CHUNK), 1), meta)
    before = seg_of(first - 1, meta)
    last = seg_of(first + CHUNK - 1, meta)
    same = (seg_col == seg_row).astype(F32)
    strict = jnp.where(row > col, same, 0.0)
    lower = jnp.where(row >= col, same, 0.0)
    carry_in = (seg_col == before).astype(F32)
    tail = (seg_col == last).astype(F32)
    whole = (last == before).astype(F32)
    return strict, lower, carry_in, tail, whole


def unit_inverse(gram):
    row = lax.broadcasted_iota(jnp.int32, (CHUNK, CHUNK), 0)
    col = lax.broadcasted_iota(jnp.int32, (CHUNK, CHUNK), 1)
    eye = (row == col).astype(F32)
    size = 8
    near = jnp.where(row // size == col // size, gram, 0.0)
    inverse = eye - near
    power = dot_nn(near, near, HIGH)
    inverse = inverse + dot_nn(inverse, power, HIGH)
    power = dot_nn(power, power, HIGH)
    inverse = inverse + dot_nn(inverse, power, HIGH)
    while size < CHUNK:
        off = (row // (2 * size) == col // (2 * size)) & (row // size != col // size)
        inverse = inverse - dot_nn(inverse, dot_nn(jnp.where(off, gram, 0.0), inverse, HIGH), HIGH)
        size *= 2
    return inverse


def silu_parts(mixed):
    sig = jax.nn.sigmoid(mixed)
    return sig, mixed * sig


def unit_parts(values):
    scale = lax.rsqrt(jnp.sum(values * values, axis=-1, keepdims=True) + EPS)
    return scale, values * scale


def delta_kernel(
    meta, eq, ek, ev, tq, tk, tv, logits,
    w_out, u_out, p_out, t_out, qe_out, m_out, mp_out, bp_out, qh_out, oh_out, mtot, btot,
):
    rows, width = w_out.shape[1:]
    head = pl.program_id(0)
    places, sames = tap_masks(meta, rows)
    q = silu_parts(conv_rows(eq, tq[0], rows, sames))[1]
    k = silu_parts(conv_rows(ek, tk[0], rows, sames))[1]
    v = silu_parts(conv_rows(ev, tv[0], rows, sames))[1]
    q = unit_parts(q)[1] * (1.0 / math.sqrt(width))
    k = unit_parts(k)[1]
    strength = jax.nn.sigmoid(pick_column(logits[...], head)) * (places < meta[2]).astype(F32)
    eye = (
        lax.broadcasted_iota(jnp.int32, (width, width), 0)
        == lax.broadcasted_iota(jnp.int32, (width, width), 1)
    ).astype(F32)
    parts = []
    for at in range(rows // CHUNK):
        here = slice(at * CHUNK, (at + 1) * CHUNK)
        strict, lower, carry_in, tail, whole = chunk_masks(meta, at)
        qc, kc, vc, bc = q[here], k[here], v[here], strength[here]
        scaled = bc * kc
        gram = dot_nt(scaled, kc, HIGH) * strict
        scores = dot_nt(qc, kc, HIGH) * lower
        inverse = unit_inverse(gram)
        both = dot_nn(inverse, jnp.concatenate([scaled, bc * vc], axis=1), HIGH)
        erase, write = both[:, :width], both[:, width:]
        carried = carry_in * erase
        state = dot_tn(kc, tail * jnp.concatenate([carried, write], axis=1), HIGH)
        step = whole * eye - state[:, :width]
        reach = dot_nn(scores, jnp.concatenate([carried, write], axis=1), HIGH)
        query = carry_in * qc - reach[:, :width]
        w_out[0, here, :] = erase
        u_out[0, here, :] = write
        p_out[0, here, :] = scores
        t_out[0, here, :] = inverse
        qe_out[0, here, :] = query
        m_out[0, here, :] = step
        parts.append((query, step, reach[:, width:], state[:, width:]))
    prefix, added = eye, jnp.zeros((width, width), F32)
    for at, (query, step, local, extra) in enumerate(parts):
        here = slice(at * CHUNK, (at + 1) * CHUNK)
        mp_out[0, here, :] = prefix
        bp_out[0, here, :] = added
        both = dot_nn(
            jnp.concatenate([query, step], axis=0), jnp.concatenate([prefix, added], axis=1), HIGH
        )
        qh_out[0, here, :] = both[:CHUNK, :width]
        oh_out[0, here, :] = both[:CHUNK, width:] + local
        prefix, added = both[CHUNK:, :width], both[CHUNK:, width:] + extra
    mtot[0] = prefix
    btot[0] = added


def hop_kernel(step, extra, state, out, *, flip):
    for head in range(step.shape[0]):
        value = state[head].astype(F32)
        product = dot_tn(step[head], value, HIGH) if flip else dot_nn(step[head], value, HIGH)
        out[head] = (product + extra[head]).astype(BF16)


def attend_kernel(meta, qh, oh, state, gain, w_own, w_oth, heads_slot, o_out, *rest):
    pieces, low = rest[:-1], rest[-1]
    heads, rows, width = qh.shape
    for head in range(heads):
        out = dot_nn(qh[head], state[head].astype(F32), HIGH) + oh[head]
        o_out[head] = out
        scale = lax.rsqrt(jnp.mean(out * out, axis=-1, keepdims=True) + EPS)
        low[:, head * width : (head + 1) * width] = (out * scale * gain[...]).astype(BF16)
    count = rows // len(pieces)
    own, oth = halves(meta, w_own.shape[0])
    for slot, piece in enumerate(pieces):
        part = low[row_of(meta, slot, count), :]
        heads_slot[pl.ds(slot * count, count), :] = part
        piece[:, own] = dot_nt(part, w_own[...]).astype(BF16)
        piece[:, oth] = dot_nt(part, w_oth[...]).astype(BF16)


def norm_two_kernel(a, b, c, d, tok, gain, hidden_out, normed_out):
    total = a[...].astype(F32) + b[...].astype(F32) + c[...].astype(F32) + d[...].astype(F32)
    hidden = tok[...].astype(F32) + total
    scale = lax.rsqrt(jnp.mean(hidden * hidden, axis=-1, keepdims=True) + EPS)
    hidden_out[...] = hidden
    normed_out[...] = (hidden * scale * gain[...]).astype(BF16)


def norm_back(grad, values, gain):
    scale = lax.rsqrt(jnp.mean(values * values, axis=-1, keepdims=True) + EPS)
    normal = values * scale
    hat = grad * gain
    back = scale * (hat - normal * jnp.mean(hat * normal, axis=-1, keepdims=True))
    return back, jnp.sum(grad * normal, axis=0, keepdims=True)


def norm_two_back_kernel(meta, a, b, c, d, hidden, cot, gain, grad_hidden, grad_att, d_gain):
    total = a[...].astype(F32) + b[...].astype(F32) + c[...].astype(F32) + d[...].astype(F32)
    back, d_gain[...] = norm_back(total, hidden[...], gain[...])
    places = meta[3] + meta[6] + lax.broadcasted_iota(jnp.int32, (hidden.shape[0], 1), 0)
    grad = cot[...].astype(F32) * (places < meta[2]).astype(F32) + back
    grad_hidden[...] = grad
    grad_att[...] = grad.astype(BF16)


def norm_one_back_kernel(a, b, c, d, tok, gain, grad_hidden, d_tok, d_gain):
    total = a[...].astype(F32) + b[...].astype(F32) + c[...].astype(F32) + d[...].astype(F32)
    back, d_gain[...] = norm_back(total, tok[...].astype(F32), gain[...])
    d_tok[...] = (grad_hidden[...] + back).astype(BF16)


def place_kernel(meta, a, b, c, d, out):
    rows = a.shape[0]
    for slot, piece in enumerate((a, b, c, d)):
        out[row_of(meta, slot, rows), :] = piece[...]


def grad_act_kernel(meta, cot, w_own, w_oth, low_out, act_out):
    rows, width = cot.shape
    slots = 4
    count = rows // slots
    for slot in range(slots):
        at = row_of(meta, slot, count)
        places = meta[3] + meta[6 + slot] + lax.broadcasted_iota(jnp.int32, (count, 1), 0)
        keep = (places < meta[2]).astype(F32)
        low_out[pl.ds(slot * count, count), :] = (cot[at, :].astype(F32) * keep).astype(BF16)
    own, oth = halves(meta, width // 2)

    @pl.loop(0, 2)
    def _(step):
        at = pl.ds(pl.multiple_of(step * (rows // 2), rows // 2), rows // 2)
        act_out[at, :] = dot_nn(low_out[at, own], w_own[...]) + dot_nn(low_out[at, oth], w_oth[...])


def ffn_kernel(meta, n0, n1, n2, n3, g_own, g_oth, u_own, u_oth, grad_act, n_out, act_out, gu_out, *pieces):
    count, width = n0.shape
    units = g_own.shape[1]
    for slot, source in enumerate((n0, n1, n2, n3)):
        n_out[pl.ds(slot * count, count), :] = source[...]
    own, oth = halves(meta, width // 2)
    for step in range(2):
        at = pl.ds(step * 2 * count, 2 * count)
        left, right = n_out[at, own], n_out[at, oth]
        gate = dot_nn(left, g_own[...]) + dot_nn(right, g_oth[...])
        up = dot_nn(left, u_own[...]) + dot_nn(right, u_oth[...])
        sig = jax.nn.sigmoid(gate)
        act_out[at, :] = (gate * sig * up).astype(BF16)
        grad = grad_act[at, :]
        grad_gate = (grad * up * sig * (1.0 + gate * (1.0 - sig))).astype(BF16)
        grad_up = (grad * gate * sig).astype(BF16)
        gu_out[at, :units] = grad_gate
        gu_out[at, units:] = grad_up
        first = (dot_nt(grad_gate, g_own[...]) + dot_nt(grad_up, u_own[...])).astype(BF16)
        pieces[2 * step][:, own] = first[:count]
        pieces[2 * step + 1][:, own] = first[count:]
        second = (dot_nt(grad_gate, g_oth[...]) + dot_nt(grad_up, u_oth[...])).astype(BF16)
        pieces[2 * step][:, oth] = second[:count]
        pieces[2 * step + 1][:, oth] = second[count:]


def down_kernel(meta, act, w_own, w_oth, *pieces):
    count = pieces[0].shape[0]
    own, oth = halves(meta, w_own.shape[0])
    first = dot_nt(act[...], w_own[...]).astype(BF16)
    for slot, piece in enumerate(pieces):
        piece[:, own] = first[slot * count : (slot + 1) * count]
    second = dot_nt(act[...], w_oth[...]).astype(BF16)
    for slot, piece in enumerate(pieces):
        piece[:, oth] = second[slot * count : (slot + 1) * count]


def heads_back_kernel(
    meta, g0, g1, g2, g3, w_own, w_oth, o_in, gain, qe, qh, grad_o, d_chunk, d_total, d_gain, cat_out, grad
):
    heads, rows, width = o_in.shape
    count = g0.shape[0]
    own, oth = halves(meta, w_own.shape[0])
    for slot, source in enumerate((g0, g1, g2, g3)):
        cat_out[pl.ds(slot * count, count), :] = source[...]
    whole = dot_nn(cat_out[:, own], w_own[...]) + dot_nn(cat_out[:, oth], w_oth[...])
    for slot in range(4):
        grad[row_of(meta, slot, count), :] = whole[slot * count : (slot + 1) * count]
    total_gain = jnp.zeros((1, width), F32)
    for head in range(heads):
        out = o_in[head]
        back, part = norm_back(grad[:, head * width : (head + 1) * width], out, gain[...])
        total_gain = total_gain + part
        grad_o[head] = back
        d_total[head] = dot_tn(qh[head], back, HIGH)
        for at in range(rows // CHUNK):
            here = slice(at * CHUNK, (at + 1) * CHUNK)
            d_chunk[head, here, :] = dot_tn(qe[head, here, :], back[here], HIGH)
    d_gain[...] = total_gain


def delta_back_kernel(
    meta, eq, ek, ev, tq, tk, tv, logits,
    w_in, u_in, p_in, t_in, m_in, mp_in, bp_in, s_in, ds_in, do_in, dc_in,
    grad_main, grad_rim, grad_tail, d_taps, d_logits, pad,
):
    rows, width = w_in.shape[1:]
    head = pl.program_id(0)
    places, sames = tap_masks(meta, rows)
    mixed = [conv_rows(e, t[0], rows, sames) for e, t in ((eq, tq), (ek, tk), (ev, tv))]
    sigs, values = zip(*[silu_parts(m) for m in mixed], strict=True)
    scale_q, unit_q = unit_parts(values[0])
    scale_k, unit_k = unit_parts(values[1])
    root = 1.0 / math.sqrt(width)
    q = unit_q * root
    k = unit_k
    v = values[2]
    keep = (places < meta[2]).astype(F32)
    sig_b = jax.nn.sigmoid(pick_column(logits[...], head))
    strength = sig_b * keep
    chunks = rows // CHUNK
    state_in = s_in[0].astype(F32)
    grads_after = [None] * chunks
    grads_after[chunks - 1] = ds_in[0].astype(F32)
    for at in range(chunks - 1, 0, -1):
        here = slice(at * CHUNK, (at + 1) * CHUNK)
        grads_after[at - 1] = dot_tn(m_in[0, here, :], grads_after[at], HIGH) + dc_in[0, here, :]
    grads_q, grads_k, grads_v, grads_b = [], [], [], []
    for at in range(chunks):
        here = slice(at * CHUNK, (at + 1) * CHUNK)
        strict, lower, carry_in, tail, whole = chunk_masks(meta, at)
        qc, kc, vc, bc = q[here], k[here], v[here], strength[here]
        erase, write, scores, inverse = w_in[0, here, :], u_in[0, here, :], p_in[0, here, :], t_in[0, here, :]
        state = dot_nn(mp_in[0, here, :], state_in, HIGH) + bp_in[0, here, :]
        grad_state = grads_after[at]
        grad_o = do_in[0, here, :]
        fresh = write - carry_in * dot_nn(erase, state, HIGH)
        d_fresh = dot_tn(scores, grad_o, HIGH) + tail * dot_nn(kc, grad_state, HIGH)
        d_scores = dot_nt(grad_o, fresh, HIGH) * lower
        back = dot_nt(jnp.concatenate([carry_in * grad_o, carry_in * d_fresh], axis=0), state, HIGH)
        d_q = back[:CHUNK] + dot_nn(d_scores, kc, HIGH)
        d_k = dot_tn(d_scores, qc, HIGH) + dot_nt(tail * fresh, grad_state, HIGH)
        d_erase = -back[CHUNK:]
        right = dot_tn(inverse, jnp.concatenate([d_erase, d_fresh], axis=1), HIGH)
        d_gram = -strict * dot_nt(right, jnp.concatenate([erase, write], axis=1), HIGH)
        d_scaled = right[:, :width] + dot_nn(d_gram, kc, HIGH)
        d_k = d_k + dot_tn(d_gram, bc * kc, HIGH) + bc * d_scaled
        d_b = jnp.sum(d_scaled * kc + right[:, width:] * vc, axis=1, keepdims=True)
        grads_q.append(d_q)
        grads_k.append(d_k)
        grads_v.append(bc * right[:, width:])
        grads_b.append(d_b)
    d_q, d_k, d_v, d_b = (jnp.concatenate(g, axis=0) for g in (grads_q, grads_k, grads_v, grads_b))
    d_logit = d_b * keep * sig_b * (1.0 - sig_b)
    lane = lax.broadcasted_iota(jnp.int32, d_logits.shape, 1)
    d_logits[...] = jnp.where(lane == head, d_logit, d_logits[...])
    d_q = root * scale_q * (d_q - unit_q * jnp.sum(d_q * unit_q, axis=-1, keepdims=True))
    d_k = scale_k * (d_k - unit_k * jnp.sum(d_k * unit_k, axis=-1, keepdims=True))
    zeros = jnp.zeros((RIM, width), F32)
    pad[pl.ds(0, RIM), :] = zeros
    pad[pl.ds(RIM + rows, RIM), :] = zeros
    heads_width = grad_main.shape[1] // 3
    for block, (ext, taps, grad) in enumerate(((eq, tq, d_q), (ek, tk, d_k), (ev, tv, d_v))):
        d_mixed = grad * sigs[block] * (1.0 + mixed[block] * (1.0 - sigs[block]))
        total = jnp.zeros((rows + RIM, width), F32)
        for j in range(TAPS):
            masked = d_mixed * sames[j]
            pad[pl.ds(RIM, rows), :] = masked
            total = total + taps[0, j : j + 1, :] * pad[pl.ds(j, rows + RIM), :]
            d_taps[block, j : j + 1, :] = jnp.sum(
                masked * ext[RIM - j : RIM - j + rows, :], axis=0, keepdims=True
            )
        lanes = pl.ds(pl.multiple_of(block * heads_width + head * width, width), width)
        grad_main[:, lanes] = total[RIM:].astype(BF16)
        grad_rim[:, lanes] = total[:RIM]
        grad_tail[:, lanes] = total[rows:]


def back_project_kernel(meta, grad, logit, wq, wk, wv, wb, xq, xk, xv, xb, *pieces):
    count = pieces[0].shape[0]
    chan = wq.shape[1]
    own, oth = halves(meta, wq.shape[0])
    for side, weights in ((own, (wq, wk, wv, wb)), (oth, (xq, xk, xv, xb))):
        total = dot_nt(logit[...], weights[3][...])
        for block in range(3):
            total = total + dot_nt(grad[:, block * chan : (block + 1) * chan], weights[block][...])
        total = total.astype(BF16)
        for slot, piece in enumerate(pieces):
            piece[:, side] = total[slot * count : (slot + 1) * count]


def flipped(value, axis, bit):
    return lax.ppermute(value, axis, [(i, i ^ bit) for i in range(lax.axis_size(axis))])


def shifted(value, axis, by, reach=None):
    length = lax.axis_size(axis)
    pairs = [(i, i + by) for i in range(length) if 0 <= i + by < length]
    if reach is not None:
        pairs = [pair for pair in pairs if reach(pair[0])]
    return lax.ppermute(value, axis, pairs)


def exchanged(pieces):
    return [pieces[0]] + [flipped(piece, "tp", slot) for slot, piece in enumerate(pieces) if slot]


def gathered(piece):
    return [piece] + [flipped(piece, "tp", slot) for slot in range(1, lax.axis_size("tp"))]


def summed(value, axis):
    bit = 1
    while bit < lax.axis_size(axis):
        value = value + flipped(value, axis, bit)
        bit *= 2
    return value


def contract_rows(left_side, right_side):
    return lax.dot_general(
        left_side, right_side, (((0,), (0,)), ((), ())), preferred_element_type=F32
    )


def pair_gradient(left, right, half):
    mine = lax.axis_index("fsdp")
    other = lax.dynamic_slice_in_dim(left, (1 - mine) * half, half, 1)
    same = lax.dynamic_slice_in_dim(left, mine * half, half, 1)
    sent = flipped(contract_rows(other, right).astype(BF16), "fsdp", 1)
    return (contract_rows(same, right) + sent.astype(F32)).astype(BF16)


def line_scatter(value):
    length = lax.axis_size("ctx")
    place = lax.axis_index("ctx")
    rows = value.shape[0] // length

    def part(index):
        return lax.dynamic_slice_in_dim(value, jnp.clip(index, 0, length - 1) * rows, rows, 0)

    right = left = None
    for step in range(length - 1):
        send = part(length - 1 - step + place)
        if right is not None:
            send = (send.astype(F32) + right.astype(F32)).astype(BF16)
        right = shifted(send, "ctx", 1, lambda i: i <= step)
        send = part(place - (length - 1) + step)
        if left is not None:
            send = (send.astype(F32) + left.astype(F32)).astype(BF16)
        left = shifted(send, "ctx", -1, lambda i: i >= length - 1 - step)
    total = part(place).astype(F32)
    if length > 1:
        total = total + right.astype(F32) + left.astype(F32)
    return total


def shards(
    tokens, seq_bounds, w_query, w_key, w_value, w_beta, conv_taps, out_gain, w_out,
    attn_gain, ffn_gain, w_gate, w_up, w_down, cotangent,
):
    rows, width = tokens.shape
    half = w_query.shape[0]
    chan = w_query.shape[1]
    heads = w_beta.shape[1]
    dim = out_gain.shape[0]
    units = w_gate.shape[1]
    slots = lax.axis_size("tp")
    count = rows // slots
    core, place, member = lax.axis_index("fsdp"), lax.axis_index("ctx"), lax.axis_index("tp")
    meta = jnp.concatenate(
        [
            seq_bounds[0],
            jnp.stack(
                [place * rows, core * half, (1 - core) * half]
                + [(member ^ slot) * count for slot in range(slots)]
            ).astype(jnp.int32),
        ]
    )
    attn_row, ffn_row, out_row = attn_gain[None, :], ffn_gain[None, :], out_gain[None, :]

    rim = shifted(tokens[rows - RIM :], "ctx", 1)
    x_query, x_key, x_value, x_beta = (flipped(w, "fsdp", 1) for w in (w_query, w_key, w_value, w_beta))
    tok_own = lax.dynamic_slice_in_dim(tokens, member * count, count, 0)
    cot_own = lax.dynamic_slice_in_dim(cotangent, member * count, count, 0)

    normed, proj, logits = call(
        project_kernel,
        [shape(rows, width, dtype=BF16), shape(rows + RIM, 3 * chan), shape(rows, heads)],
        (meta, tokens, rim, attn_row, w_query, w_key, w_value, w_beta, x_query, x_key, x_value, x_beta),
        flops=2 * rows * width * 3 * chan,
        scratch=[VMEM((rows + RIM, width), BF16)],
    )
    ext_specs = [
        pl.BlockSpec((rows + RIM, dim), functools.partial(lambda b, h: (0, b * heads + h), b))
        for b in range(3)
    ]
    tap_specs = [
        pl.BlockSpec((1, TAPS, dim), functools.partial(lambda b, h: (b, 0, h), b)) for b in range(3)
    ]
    per_head = pl.BlockSpec((1, rows, dim), lambda h: (h, 0, 0))
    per_state = pl.BlockSpec((1, dim, dim), lambda h: (h, 0, 0))
    logit_spec = pl.BlockSpec((rows, heads), lambda h: (0, 0))
    tall, square = shape(heads, rows, dim), shape(heads, dim, dim)
    erase, write, scores, inverse, query_eff, step, prefix, added, query_hat, out_hat, m_total, b_total = call(
        delta_kernel,
        [tall] * 10 + [square] * 2,
        (meta, proj, proj, proj, conv_taps, conv_taps, conv_taps, logits),
        flops=heads * 60 * rows * dim * dim,
        grid=(heads,),
        in_specs=[SCALARS] + ext_specs + tap_specs + [logit_spec],
        out_specs=[per_head] * 10 + [per_state] * 2,
    )

    def hop(matrix, extra, state, flip):
        return call(
            functools.partial(hop_kernel, flip=flip),
            shape(heads, dim, dim, dtype=BF16),
            (matrix, extra, state),
            flops=2 * heads * dim**3,
            in_specs=[WHOLE] * 3,
        )

    state = jnp.zeros((heads, dim, dim), BF16)
    for index in range(lax.axis_size("ctx") - 1):
        sent = b_total.astype(BF16) if index == 0 else hop(m_total, b_total, state, False)
        state = shifted(sent, "ctx", 1)

    x_out = flipped(w_out, "fsdp", 1)
    piece_shape = shape(count, width, dtype=BF16)
    heads_slot, heads_out, *pieces = call(
        attend_kernel,
        [shape(rows, chan, dtype=BF16), tall] + [piece_shape] * slots,
        (meta, query_hat, out_hat, state, out_row, w_out, x_out),
        flops=2 * rows * width * chan,
        scratch=[VMEM((rows, chan), BF16)],
    )
    x_down, x_gate, x_up = (flipped(w, "fsdp", 1) for w in (w_down, w_gate, w_up))
    grad_low, grad_act = call(
        grad_act_kernel,
        [shape(rows, width, dtype=BF16), shape(rows, units)],
        (meta, cotangent, w_down, x_down),
        flops=2 * rows * width * units,
    )
    hidden, normed_two = call(
        norm_two_kernel,
        [shape(count, width), piece_shape],
        (*exchanged(pieces), tok_own, ffn_row),
        in_specs=[WHOLE] * 6,
    )
    normed_slot, act, grad_gu, *pieces = call(
        ffn_kernel,
        [
            shape(rows, width, dtype=BF16),
            shape(rows, units, dtype=BF16),
            shape(rows, 2 * units, dtype=BF16),
        ]
        + [piece_shape] * slots,
        (meta, *gathered(normed_two), w_gate, x_gate, w_up, x_up, grad_act),
        flops=8 * rows * width * units,
    )
    received = exchanged(pieces)
    down_pair = pair_gradient(grad_low, act, half)
    gu_pair = pair_gradient(normed_slot, grad_gu, half)
    grad_hidden, grad_att, d_ffn_part = call(
        norm_two_back_kernel,
        [shape(count, width), piece_shape, shape(1, width)],
        (meta, *received, hidden, cot_own, ffn_row),
    )
    down_pieces = call(
        down_kernel,
        [piece_shape] * slots,
        (meta, act, w_down, x_down),
        flops=2 * rows * width * units,
    )
    grad_o, d_chunk, d_total, d_head_part, grad_att_slot = call(
        heads_back_kernel,
        [tall, tall, square, shape(1, dim), shape(rows, width, dtype=BF16)],
        (meta, *gathered(grad_att), w_out, x_out, heads_out, out_row, query_eff, query_hat),
        flops=2 * rows * width * chan,
        scratch=[VMEM((rows, chan), F32)],
    )
    grad_state = jnp.zeros((heads, dim, dim), BF16)
    for index in range(lax.axis_size("ctx") - 1):
        sent = d_total.astype(BF16) if index == 0 else hop(m_total, d_total, grad_state, True)
        grad_state = shifted(sent, "ctx", -1)
    out_pair = pair_gradient(grad_att_slot, heads_slot, half)

    grad_main, grad_rim, grad_tail, d_conv_part, d_logits = call(
        delta_back_kernel,
        [
            shape(rows, 3 * chan, dtype=BF16),
            shape(RIM, 3 * chan),
            shape(RIM, 3 * chan),
            shape(3, TAPS, chan),
            shape(rows, heads),
        ],
        (
            meta, proj, proj, proj, conv_taps, conv_taps, conv_taps, logits,
            erase, write, scores, inverse, step, prefix, added, state, grad_state, grad_o, d_chunk,
        ),
        flops=heads * 60 * rows * dim * dim,
        grid=(heads,),
        in_specs=[SCALARS] + ext_specs + tap_specs + [logit_spec] + [per_head] * 7 + [per_state] * 2 + [per_head] * 2,
        out_specs=[
            pl.BlockSpec((rows, 3 * chan), lambda h: (0, 0)),
            pl.BlockSpec((RIM, 3 * chan), lambda h: (0, 0)),
            pl.BlockSpec((RIM, 3 * chan), lambda h: (0, 0)),
            pl.BlockSpec((3, TAPS, dim), lambda h: (0, 0, h)),
            pl.BlockSpec((rows, heads), lambda h: (0, 0)),
        ],
        scratch=[VMEM((rows + 2 * RIM, dim), F32)],
    )
    tail = (grad_tail + shifted(grad_rim, "ctx", -1)).astype(BF16)
    grad_proj = lax.dynamic_update_slice(grad_main, tail, (rows - RIM, 0))
    grad_logit = d_logits.astype(BF16)
    ordered = jnp.concatenate(
        [
            lax.dynamic_slice_in_dim(grad_proj, (member ^ slot) * count, count, 0)
            for slot in range(slots)
        ],
        axis=0,
    )
    ordered_logit = jnp.concatenate(
        [
            lax.dynamic_slice_in_dim(grad_logit, (member ^ slot) * count, count, 0)
            for slot in range(slots)
        ],
        axis=0,
    )
    pieces = call(
        back_project_kernel,
        [piece_shape] * slots,
        (meta, ordered, ordered_logit, w_query, w_key, w_value, w_beta, x_query, x_key, x_value, x_beta),
        flops=2 * rows * width * 3 * chan,
    )
    d_tok_own, d_attn_part = call(
        norm_one_back_kernel,
        [piece_shape, shape(1, width)],
        (*exchanged(pieces), tok_own, attn_row, grad_hidden),
        in_specs=[WHOLE] * 7,
    )
    d_tokens = call(place_kernel, shape(rows, width, dtype=BF16), (meta, *gathered(d_tok_own)))
    proj_pair = pair_gradient(normed, grad_proj, half)

    down_sum = hidden
    for piece in exchanged(down_pieces):
        down_sum = down_sum + piece.astype(F32)
    out = call(place_kernel, shape(rows, width, dtype=BF16), (meta, *gathered(down_sum.astype(BF16))))

    d_w_down = line_scatter(down_pair)
    d_w_gu = line_scatter(gu_pair)
    d_w_out = line_scatter(out_pair)
    d_w_proj = line_scatter(proj_pair)

    d_beta_part = contract_rows(grad_logit, normed)
    conv_rows_count = 3 * TAPS * chan // width
    early = summed(
        jnp.concatenate([d_ffn_part, jnp.pad(d_head_part, ((0, 0), (0, width - dim)))], axis=0), "tp"
    )
    bundle = jnp.concatenate([early, d_beta_part, d_conv_part.reshape(conv_rows_count, width)], axis=0)
    bundle = summed(summed(bundle, "fsdp"), "ctx")
    d_attn = summed(summed(summed(d_attn_part, "tp"), "fsdp"), "ctx")
    share = width // (lax.axis_size("fsdp") * lax.axis_size("ctx"))
    d_beta = lax.dynamic_slice_in_dim(
        bundle[2 : 2 + heads], core * half + place * share, share, 1
    ).T
    return (
        out,
        d_tokens,
        d_w_proj[:, :chan],
        d_w_proj[:, chan : 2 * chan],
        d_w_proj[:, 2 * chan :],
        d_beta,
        bundle[2 + heads :].reshape(3, TAPS, chan),
        bundle[1, :dim],
        d_w_out,
        d_attn[0],
        bundle[0],
        d_w_gu[:, :units],
        d_w_gu[:, units:],
        d_w_down,
    )


def solution(mesh):
    both = P(("fsdp", "ctx"), None)
    weight = P("fsdp", "tp")
    grad = P(("fsdp", "ctx"), "tp")
    in_specs = (
        both, P("fsdp", None), weight, weight, weight, weight, P(None, None, "tp"), P(), weight,
        P(), P(), weight, weight, weight, both,
    )
    out_specs = (
        both, both, grad, grad, grad, grad, P(None, None, "tp"), P(), grad, P(), P(), grad, grad, grad,
    )
    return jax.shard_map(shards, mesh=mesh, in_specs=in_specs, out_specs=out_specs, check_vma=False)
```

time: 2340 us -> 729 us (0.31)
  other arithmetic: 752 us -> 28.2 us
  waiting for transfers between devices: 773 us -> 240 us
  matrix products: 470 us -> 28.9 us
  Pallas kernels: 0 us -> 199 us
  local copies, waits for them, and re-layouts: 220 us -> 24.7 us
  starting transfers between devices: 25.5 us -> 194 us
  blocking collectives: 40.9 us -> 0 us
    another operation x111 -> x0, other arithmetic: 525 us -> none  [the longest x104 525 us: group_parts(): jax.scipy.linalg.solve_triangular(system, right_hand, lower=True, unit_di...]
    reduce_scatter x7 -> x0, waiting for transfers between devices: 463 us -> none  [the longest x1 118 us: shards(): lax.psum_scatter(d_w_down.astype(jnp.bfloat16), ('fsdp', 'ctx'), scatter_...]
    dot_general x227 -> x0, matrix products: 389 us -> none  [the longest x206 301 us: inner(): jnp.einsum(form, left_side, right_side, precision=HIGH, preferred_element...]
    psum x3 -> x0, waiting for transfers between devices: 237 us -> none  [the longest x1 107 us: shards(): lax.psum(partial_down.astype(jnp.bfloat16), 'tp').astype(jnp.float32)]
    ppermute x8 -> x78, waiting for transfers between devices: 25.2 us -> 240 us  [the longest x32 137 us: shifted(): return lax.ppermute(value, axis, pairs)]
    pallas_call x0 -> x18, Pallas kernels: none -> 199 us  [call(): pl.pallas_call(kernel, out_shape=out_shape, in_specs=in_specs or [SCALARS...]
    ppermute x8 -> x78, starting transfers between devices: 23.7 us -> 194 us  [the longest x46 121 us: flipped(): lax.ppermute(value, axis, [(i, i ^ bit) for i in range(lax.axis_size(axis...]
    dynamic_update_slice x48 -> x1, other arithmetic: 65.5 us -> 1.52 us  [shards(): grad_proj = lax.dynamic_update_slice(grad_main, tail, (rows - RIM, 0))]
  transfers between devices with their start and end apart: 26 -> 78, of which waited for: 19 -> 30; matrix products, arithmetic and copies ran while one was open for 38% -> 10% of each run, Pallas kernels for 0% -> 25%
where the time goes in v1:
time: 729 us; the launch traced here: 717 us
  waiting for transfers between devices  240 us (33%)
  Pallas kernels  199 us (27%)
  starting transfers between devices  194 us (27%)
  matrix products  28.9 us (4%)
  other arithmetic  28.2 us (4%)
  local copies, waits for them, and re-layouts  24.7 us (3%)
    pallas_call x18, Pallas kernels, call(): pl.pallas_call(kernel, out_shape=out_shape, in_specs=in_specs or [SCALARS...  199 us
    ppermute x32, waiting for transfers between devices, shifted(): return lax.ppermute(value, axis, pairs)  137 us
    ppermute x46, starting transfers between devices, flipped(): lax.ppermute(value, axis, [(i, i ^ bit) for i in range(lax.axis_size(axis...  121 us
    ppermute x46, waiting for transfers between devices, flipped(): lax.ppermute(value, axis, [(i, i ^ bit) for i in range(lax.axis_size(axis...  103 us
    ppermute x32, starting transfers between devices, shifted(): return lax.ppermute(value, axis, pairs)  73 us
    dot_general x9, matrix products, contract_rows(): lax.dot_general(left_side, right_side, (((0,), (0,)), ((), ())), preferre...  28.9 us
  transfers between devices with their start and end apart: 78, of which 30 were waited for; matrix products, arithmetic and copies ran while one was open for 10% of the time, Pallas kernels for 25%

profile of v1, /device:TPU:16, one launch (start us, length us, event | category | flops | bytes accessed | tf_op | source)
XLA Modules:
  0.0 716.6 jit_solution(4565693604879361402)
XLA Ops:
  15.3 10.6 %shard_map.254 = (bf16[512,2048]{1,0:T(8,128)(2,1)}, f32[528,1536]{1,0:T(8,128)}, f32[512,4]{1,0:T(8,128)}) custom-call(s32[10]{0:T(128)} %concatenate.15.meta, bf16[512,2048]{1,0:T(8,128)(2,1)} %tok.1, bf16[16,2048]{1,0:T(8,128)(2,1)} %copy-done.50, f32[1,2048]{1,0:T(1,128)} %bitcast.36, bf16[1024,512]{1,0:T(8,128)(2,1)} %wq.3, bf16[1024,512]{1,0:T(8,128)(2,1)} %wk.3, ...), custom_call_target="tpu_custom_call" | custom-call | flops 3221225472 | bytes 13828136 | tf_op jit(solution)/shard_map/pallas_call | solution.py:46
  26.0 64.5 %shard_map.255 = (f32[4,512,128]{2,1,0:T(8,128)}, f32[4,512,128]{2,1,0:T(8,128)}, f32[4,512,128]{2,1,0:T(8,128)}, f32[4,512,128]{2,1,0:T(8,128)}, f32[4,512,128]...) custom-call(s32[10]{0:T(128)} %concatenate.15.meta, ...), custom_call_target="tpu_custom_call" | custom-call | flops 2013265920 | bytes 20824104 | tf_op jit(solution)/shard_map/pallas_call | solution.py:46
  119.5 7.0 shard_map.258
  129.5 8.6 %collective-permute-done.9.b = bf16[128,2048]{1,0:T(8,128)(2,1)S(1)} collective-permute-done((bf16[128,2048]{1,0:T(8,128)(2,1)}, bf16[128,2048]{1,0:T(8,128)(2,1)S(1)}, u32[]{:S(2)}, u32[]{:S(2)}) %collective-permute-start.9) | collective-permute-done | bytes 524320 | tf_op jit(solution)/shard_map/ppermute | solution.py:446
  143.1 7.5 %collective-permute-done.10.c = bf16[128,2048]{1,0:T(8,128)(2,1)S(1)} collective-permute-done((bf16[128,2048]{1,0:T(8,128)(2,1)}, bf16[128,2048]{1,0:T(8,128)(2,1)S(1)}, u32[]{:S(2)}, u32[]{:S(2)}) %collective-permute-start.10) | collective-permute-done | bytes 524320 | tf_op jit(solution)/shard_map/ppermute | solution.py:446
  160.1 9.0 %shard_map.260 = (bf16[512,2048]{1,0:T(8,128)(2,1)}, f32[512,1408]{1,0:T(8,128)}) custom-call(s32[10]{0:T(128)} %concatenate.15.meta, bf16[512,2048]{1,0:T(8,128)(2,1)} %cot.1, bf16[1024,1408]{1,0:T(8,128)(2,1)} %w_own.6, bf16[1024,1408]{1,0:T(8,128)(2,1)} %collective-permute-done.17.w_oth), custom_call_target="tpu_custom_call" | custom-call | flops 2952790016 | bytes 12845096 | tf_op jit(solution)/shard_map/pallas_call | solution.py:46
  169.8 7.4 %collective-permute-done.13.n2 = bf16[128,2048]{1,0:T(8,128)(2,1)S(1)} collective-permute-done((bf16[128,2048]{1,0:T(8,128)(2,1)}, bf16[128,2048]{1,0:T(8,128)(2,1)S(1)}, u32[]{:S(2)}, u32[]{:S(2)}) %collective-permute-start.13) | collective-permute-done | bytes 524320 | tf_op jit(solution)/shard_map/ppermute | solution.py:446
  178.1 20.5 %shard_map.261 = (bf16[512,2048]{1,0:T(8,128)(2,1)}, bf16[512,1408]{1,0:T(8,128)(2,1)}, bf16[512,2816]{1,0:T(8,128)(2,1)}, bf16[128,2048]{1,0:T(8,128)(2,1)}, bf...) custom-call(s32[10]{0:T(128)} %concatenate.15.meta, ...), custom_call_target="tpu_custom_call" | custom-call | flops 11811160064 | bytes 25034792 | tf_op jit(solution)/shard_map/pallas_call | solution.py:46
  199.3 8.1 %shard_map.262 = (bf16[128,2048]{1,0:T(8,128)(2,1)}, bf16[128,2048]{1,0:T(8,128)(2,1)}, bf16[128,2048]{1,0:T(8,128)(2,1)}, bf16[128,2048]{1,0:T(8,128)(2,1)}) custom-call(s32[10]{0:T(128)} %concatenate.15.meta, bf16[512,1408]{1,0:T(8,128)(2,1)} %get-tuple-element.82.act, bf16[1024,1408]{1,0:T(8,128)(2,1)} %w_own.6, ...), custom_call_target="tpu_custom_call" | custom-call | flops 2952790016 | bytes 9306152 | tf_op jit(solution)/shard_map/pallas_call | solution.py:46
  223.9 26.1 %collective-permute-done.25.c = bf16[128,2048]{1,0:T(8,128)(2,1)S(1)} collective-permute-done((bf16[128,2048]{1,0:T(8,128)(2,1)S(1)}, bf16[128,2048]{1,0:T(8,128)(2,1)S(1)}, u32[]{:S(2)}, u32[]{:S(2)}) %collective-permute-start.25) | collective-permute-done | bytes 524320 | tf_op jit(solution)/shard_map/ppermute | solution.py:446
  259.1 11.1 %collective-permute-done.27.g1 = bf16[128,2048]{1,0:T(8,128)(2,1)S(1)} collective-permute-done((bf16[128,2048]{1,0:T(8,128)(2,1)}, bf16[128,2048]{1,0:T(8,128)(2,1)S(1)}, u32[]{:S(2)}, u32[]{:S(2)}) %collective-permute-start.27) | collective-permute-done | bytes 524320 | tf_op jit(solution)/shard_map/ppermute | solution.py:446
  271.9 10.3 %collective-permute-done.28.g2 = bf16[128,2048]{1,0:T(8,128)(2,1)S(1)} collective-permute-done((bf16[128,2048]{1,0:T(8,128)(2,1)}, bf16[128,2048]{1,0:T(8,128)(2,1)S(1)}, u32[]{:S(2)}, u32[]{:S(2)}) %collective-permute-start.28) | collective-permute-done | bytes 524320 | tf_op jit(solution)/shard_map/ppermute | solution.py:446
  283.2 8.7 %shard_map.265 = (f32[4,512,128]{2,1,0:T(8,128)}, f32[4,512,128]{2,1,0:T(8,128)}, f32[4,128,128]{2,1,0:T(8,128)}, f32[1,128]{1,0:T(1,128)}, bf16[512,2048]{1,0:T(8,128)(2,1)}) custom-call(s32[10]{0:T(128)} %concatenate.15.meta, bf16[128,2048]{1,0:T(8,128)(2,1)} %get-tuple-element.98.g0, bf16[128,2048]{1,0:T(8,128)(2,1)} %copy-done.27, ...), custom_call_target="tpu_custom_call" | custom-call | flops 1073741824 | bytes 11797544 | tf_op jit(solution)/shard_map/pallas_call | solution.py:46
  320.5 35.9 %shard_map.268 = (bf16[512,1536]{1,0:T(8,128)(2,1)}, f32[16,1536]{1,0:T(8,128)}, f32[16,1536]{1,0:T(8,128)}, f32[3,4,512]{2,1,0:T(4,128)}, f32[512,4]{1,0:T(8,128)}) custom-call(s32[10]{0:T(128)} %concatenate.15.meta, f32[528,1536]{1,0:T(8,128)} %get-tuple-element.69.eq.ek.ev, f32[528,1536]{1,0:T(8,128)} %get-tuple-element.69.eq.ek.ev, ...), custom_call_target="tpu_custom_call" | custom-call | flops 2013265920 | bytes 21315624 | tf_op jit(solution)/shard_map/pallas_call | solution.py:46
  368.5 8.8 %shard_map.269 = (bf16[128,2048]{1,0:T(8,128)(2,1)}, bf16[128,2048]{1,0:T(8,128)(2,1)}, bf16[128,2048]{1,0:T(8,128)(2,1)}, bf16[128,2048]{1,0:T(8,128)(2,1)}) custom-call(s32[10]{0:T(128)} %concatenate.15.meta, bf16[512,1536]{1,0:T(8,128)(2,1)} %pad_maximum_fusion.grad, bf16[512,4]{1,0:T(8,128)(2,1)} %pad_maximum_fusion.1.logit, bf16[1024,512]{1,0:T(8,128)(2,1)} %wq.3, ...), custom_call_target="tpu_custom_call" | custom-call | flops 3221225472 | bytes 9981992 | tf_op jit(solution)/shard_map/pallas_call | solution.py:46
  381.4 9.4 %collective-permute-done.34.b = bf16[128,2048]{1,0:T(8,128)(2,1)S(1)} collective-permute-done((bf16[128,2048]{1,0:T(8,128)(2,1)}, bf16[128,2048]{1,0:T(8,128)(2,1)S(1)}, u32[]{:S(2)}, u32[]{:S(2)}) %collective-permute-start.34) | collective-permute-done | bytes 524320 | tf_op jit(solution)/shard_map/ppermute | solution.py:446
  404.0 8.5 %collective-permute-done.59 = f32[1,2048]{1,0:T(1,128)S(1)} collective-permute-done((f32[1,2048]{1,0:T(1,128)}, f32[1,2048]{1,0:T(1,128)S(1)}, u32[]{:S(2)}, u32[]{:S(2)}) %collective-permute-start.59) | collective-permute-done | bytes 8224 | tf_op jit(solution)/shard_map/ppermute | solution.py:446
  459.7 12.5 %collective-permute-done.75 = bf16[256,1408]{1,0:T(8,128)(2,1)S(1)} collective-permute-done((bf16[256,1408]{1,0:T(8,128)(2,1)S(1)}, bf16[256,1408]{1,0:T(8,128)(2,1)S(1)}, u32[]{:S(2)}, u32[]{:S(2)}) %collective-permute-start.75) | collective-permute-done | bytes 720928 | tf_op jit(solution)/shard_map/ppermute | solution.py:454
  477.8 77.6 %collective-permute-start.63 = (f32[1,2048]{1,0:T(1,128)S(1)}, f32[1,2048]{1,0:T(1,128)S(1)}, u32[]{:S(2)}, u32[]{:S(2)}) collective-permute-start(f32[1,2048]{1,0:T(1,128)S(1)} %add.291), channel_id=1, source_target_pairs={{0,8},{4,12},{8,0},{12,4},{1,9},{5,13},{9,1},{13,5},{2,10},{6,14},... | collective-permute-start | bytes 24584 | tf_op jit(solution)/shard_map/ppermute | solution.py:446
  566.5 11.5 %collective-permute-done.44 = bf16[256,1536]{1,0:T(8,128)(2,1)S(1)} collective-permute-done((bf16[256,1536]{1,0:T(8,128)(2,1)S(1)}, bf16[256,1536]{1,0:T(8,128)(2,1)S(1)}, u32[]{:S(2)}, u32[]{:S(2)}) %collective-permute-start.44) | collective-permute-done | bytes 786464 | tf_op jit(solution)/shard_map/ppermute | solution.py:454
  606.0 41.0 %collective-permute-done.45 = bf16[256,1536]{1,0:T(8,128)(2,1)} collective-permute-done((bf16[256,1536]{1,0:T(8,128)(2,1)}, bf16[256,1536]{1,0:T(8,128)(2,1)}, u32[]{:S(2)}, u32[]{:S(2)}) %collective-permute-start.45) | collective-permute-done | bytes 786464 | tf_op jit(solution)/shard_map/ppermute | solution.py:454
  673.0 11.8 %collective-permute-done.46 = bf16[256,1536]{1,0:T(8,128)(2,1)S(1)} collective-permute-done((bf16[256,1536]{1,0:T(8,128)(2,1)S(1)}, bf16[256,1536]{1,0:T(8,128)(2,1)S(1)}, u32[]{:S(2)}, u32[]{:S(2)}) %collective-permute-start.46) | collective-permute-done | bytes 786464 | tf_op jit(solution)/shard_map/ppermute | solution.py:454
  687.4 12.1 %collective-permute-done.67 = bf16[256,2816]{1,0:T(8,128)(2,1)S(1)} collective-permute-done((bf16[256,2816]{1,0:T(8,128)(2,1)S(1)}, bf16[256,2816]{1,0:T(8,128)(2,1)S(1)}, u32[]{:S(2)}, u32[]{:S(2)}) %collective-permute-start.67) | collective-permute-done | bytes 1441824 | tf_op jit(solution)/shard_map/ppermute | solution.py:454
  699.6 14.4 %collective-permute-done.70 = bf16[256,2816]{1,0:T(8,128)(2,1)S(1)} collective-permute-done((bf16[256,2816]{1,0:T(8,128)(2,1)S(1)}, bf16[256,2816]{1,0:T(8,128)(2,1)S(1)}, u32[]{:S(2)}, u32[]{:S(2)}) %collective-permute-start.70) | collective-permute-done | bytes 1441824 | tf_op jit(solution)/shard_map/ppermute | solution.py:454
  (333 shorter events, 271.7 us)
Async XLA Ops:
  1.3 155.5 %collective-permute-start.17 = (bf16[1024,1408]{1,0:T(8,128)(2,1)}, bf16[1024,1408]{1,0:T(8,128)(2,1)}, u32[]{:S(2)}, u32[]{:S(2)}) collective-permute-start(bf16[1024,1408]{1,0:T(8,128)(2,1)} %w_own.6), channel_id=1, source_target_pairs={{0,16},{16,0},{1,17},{17,1},{2,18},{18,2},{3,19},{19,3},{4,20},{20... | collective-permute-start | bytes 8650760 | tf_op jit(solution)/shard_map/ppermute | solution.py:446
  13.3 163.9 %collective-permute-start.15 = (bf16[1024,1408]{1,0:T(8,128)(2,1)}, bf16[1024,1408]{1,0:T(8,128)(2,1)}, u32[]{:S(2)}, u32[]{:S(2)}) collective-permute-start(bf16[1024,1408]{1,0:T(8,128)(2,1)} %g_own.1), channel_id=1, source_target_pairs={{0,16},{16,0},{1,17},{17,1},{2,18},{18,2},{3,19},{19,3},{4,20},{20... | collective-permute-start | bytes 8650760 | tf_op jit(solution)/shard_map/ppermute | solution.py:446
  13.3 163.9 %collective-permute-start.16 = (bf16[1024,1408]{1,0:T(8,128)(2,1)}, bf16[1024,1408]{1,0:T(8,128)(2,1)}, u32[]{:S(2)}, u32[]{:S(2)}) collective-permute-start(bf16[1024,1408]{1,0:T(8,128)(2,1)} %u_own.1), channel_id=1, source_target_pairs={{0,16},{16,0},{1,17},{17,1},{2,18},{18,2},{3,19},{19,3},{4,20},{20... | collective-permute-start | bytes 8650760 | tf_op jit(solution)/shard_map/ppermute | solution.py:446
  13.8 101.9 %collective-permute-start.8 = (bf16[1024,512]{1,0:T(8,128)(2,1)}, bf16[1024,512]{1,0:T(8,128)(2,1)S(1)}, u32[]{:S(2)}, u32[]{:S(2)}) collective-permute-start(bf16[1024,512]{1,0:T(8,128)(2,1)} %w_own.7), channel_id=1, source_target_pairs={{0,16},{16,0},{1,17},{17,1},{2,18},{18,2},{3,19},{19,3},{4,20},{20... | collective-permute-start | bytes 3145736 | tf_op jit(solution)/shard_map/ppermute | solution.py:446
  207.4 47.8 %collective-permute-start.20 = (bf16[128,2048]{1,0:T(8,128)(2,1)}, bf16[128,2048]{1,0:T(8,128)(2,1)S(1)}, u32[]{:S(2)}, u32[]{:S(2)}) collective-permute-start(bf16[128,2048]{1,0:T(8,128)(2,1)} %get-tuple-element.86), channel_id=1, source_target_pairs={{0,3},{1,2},{2,1},{3,0},{4,7},{5,6},{6,5},{7,4},{8,11},{9,10},{10,... | collective-permute-start | bytes 1572872 | tf_op jit(solution)/shard_map/ppermute | solution.py:446
  208.4 48.5 %collective-permute-start.19 = (bf16[128,2048]{1,0:T(8,128)(2,1)}, bf16[128,2048]{1,0:T(8,128)(2,1)S(1)}, u32[]{:S(2)}, u32[]{:S(2)}) collective-permute-start(bf16[128,2048]{1,0:T(8,128)(2,1)} %get-tuple-element.85), channel_id=1, source_target_pairs={{0,2},{1,3},{2,0},{3,1},{4,6},{5,7},{6,4},{7,5},{8,10},{9,11},{10,... | collective-permute-start | bytes 1572872 | tf_op jit(solution)/shard_map/ppermute | solution.py:446
  210.3 47.5 %collective-permute-start.18 = (bf16[128,2048]{1,0:T(8,128)(2,1)}, bf16[128,2048]{1,0:T(8,128)(2,1)S(1)}, u32[]{:S(2)}, u32[]{:S(2)}) collective-permute-start(bf16[128,2048]{1,0:T(8,128)(2,1)} %get-tuple-element.84), channel_id=1, source_target_pairs={{0,1},{1,0},{2,3},{3,2},{4,5},{5,4},{6,7},{7,6},{8,9},{9,8},{10,11... | collective-permute-start | bytes 1572872 | tf_op jit(solution)/shard_map/ppermute | solution.py:446
  210.9 39.1 %collective-permute-start.25 = (bf16[128,2048]{1,0:T(8,128)(2,1)S(1)}, bf16[128,2048]{1,0:T(8,128)(2,1)S(1)}, u32[]{:S(2)}, u32[]{:S(2)}) collective-permute-start(bf16[128,2048]{1,0:T(8,128)(2,1)S(1)} %copy-done.48), channel_id=1, source_target_pairs={{0,2},{1,3},{2,0},{3,1},{4,6},{5,7},{6,4},{7,5},{8,10},{9,11},{10,... | collective-permute-start | bytes 1572872 | tf_op jit(solution)/shard_map/ppermute | solution.py:446
  250.0 185.8 %collective-permute-start.64 = (bf16[1024,2816]{1,0:T(8,128)(2,1)}, bf16[1024,2816]{1,0:T(8,128)(2,1)}, u32[]{:S(2)}, u32[]{:S(2)}) collective-permute-start(bf16[1024,2816]{1,0:T(8,128)(2,1)} %convolution_convert_fusion), channel_id=1, source_target_pairs={{0,16},{16,0},{1,17},{17,1},{2,18},{18,2},{3,19},{19,3},{4,20},{20... | collective-permute-start | bytes 17301512 | tf_op jit(solution)/shard_map/ppermute | solution.py:446
  250.0 181.0 %collective-permute-start.71 = (bf16[1024,1408]{1,0:T(8,128)(2,1)}, bf16[1024,1408]{1,0:T(8,128)(2,1)}, u32[]{:S(2)}, u32[]{:S(2)}) collective-permute-start(bf16[1024,1408]{1,0:T(8,128)(2,1)} %convolution_convert_fusion.1), channel_id=1, source_target_pairs={{0,16},{16,0},{1,17},{17,1},{2,18},{18,2},{3,19},{19,3},{4,20},{20... | collective-permute-start | bytes 8650760 | tf_op jit(solution)/shard_map/ppermute | solution.py:446
  270.2 107.1 %collective-permute-start.21 = (bf16[128,2048]{1,0:T(8,128)(2,1)S(1)}, bf16[128,2048]{1,0:T(8,128)(2,1)S(1)}, u32[]{:S(2)}, u32[]{:S(2)}) collective-permute-start(bf16[128,2048]{1,0:T(8,128)(2,1)S(1)} %add_convert_fusion.16.a), channel_id=1, source_target_pairs={{0,1},{1,0},{2,3},{3,2},{4,5},{5,4},{6,7},{7,6},{8,9},{9,8},{10,11... | collective-permute-start | bytes 1572872 | tf_op jit(solution)/shard_map/ppermute | solution.py:446
  309.7 69.8 %collective-permute-start.22 = (bf16[128,2048]{1,0:T(8,128)(2,1)S(1)}, bf16[128,2048]{1,0:T(8,128)(2,1)S(1)}, u32[]{:S(2)}, u32[]{:S(2)}) collective-permute-start(bf16[128,2048]{1,0:T(8,128)(2,1)S(1)} %add_convert_fusion.16.a), channel_id=1, source_target_pairs={{0,2},{1,3},{2,0},{3,1},{4,6},{5,7},{6,4},{7,5},{8,10},{9,11},{10,... | collective-permute-start | bytes 1572872 | tf_op jit(solution)/shard_map/ppermute | solution.py:446
  453.1 102.5 %collective-permute-start.68 = (bf16[256,2816]{1,0:T(8,128)(2,1)S(1)}, bf16[256,2816]{1,0:T(8,128)(2,1)S(1)}, u32[]{:S(2)}, u32[]{:S(2)}) collective-permute-start(bf16[256,2816]{1,0:T(8,128)(2,1)S(1)} %get-tuple-element.127), channel_id=1, source_target_pairs={{12,8},{13,9},{14,10},{15,11},{28,24},{29,25},{30,26},{31,27}} | collective-permute-start | bytes 4325384 | tf_op jit(solution)/shard_map/ppermute | solution.py:454
  456.8 100.2 %collective-permute-start.66 = (bf16[256,2816]{1,0:T(8,128)(2,1)S(1)}, bf16[256,2816]{1,0:T(8,128)(2,1)S(1)}, u32[]{:S(2)}, u32[]{:S(2)}) collective-permute-start(bf16[256,2816]{1,0:T(8,128)(2,1)S(1)} %add_convert_fusion.6), channel_id=1, source_target_pairs={{0,4},{4,8},{1,5},{5,9},{2,6},{6,10},{3,7},{7,11},{16,20},{20,24},... | collective-permute-start | bytes 4325384 | tf_op jit(solution)/shard_map/ppermute | solution.py:454
  472.2 89.7 %collective-permute-start.37 = (bf16[128,2048]{1,0:T(8,128)(2,1)}, bf16[128,2048]{1,0:T(8,128)(2,1)S(1)}, u32[]{:S(2)}, u32[]{:S(2)}) collective-permute-start(bf16[128,2048]{1,0:T(8,128)(2,1)} %get-tuple-element.113.a), channel_id=1, source_target_pairs={{0,1},{1,0},{2,3},{3,2},{4,5},{5,4},{6,7},{7,6},{8,9},{9,8},{10,11... | collective-permute-start | bytes 1572872 | tf_op jit(solution)/shard_map/ppermute | solution.py:446
  475.3 108.2 %collective-permute-start.38 = (bf16[128,2048]{1,0:T(8,128)(2,1)}, bf16[128,2048]{1,0:T(8,128)(2,1)S(1)}, u32[]{:S(2)}, u32[]{:S(2)}) collective-permute-start(bf16[128,2048]{1,0:T(8,128)(2,1)} %get-tuple-element.113.a), channel_id=1, source_target_pairs={{0,2},{1,3},{2,0},{3,1},{4,6},{5,7},{6,4},{7,5},{8,10},{9,11},{10,... | collective-permute-start | bytes 1572872 | tf_op jit(solution)/shard_map/ppermute | solution.py:446
  477.8 82.8 %collective-permute-start.63 = (f32[1,2048]{1,0:T(1,128)S(1)}, f32[1,2048]{1,0:T(1,128)S(1)}, u32[]{:S(2)}, u32[]{:S(2)}) collective-permute-start(f32[1,2048]{1,0:T(1,128)S(1)} %add.291), channel_id=1, source_target_pairs={{0,8},{4,12},{8,0},{12,4},{1,9},{5,13},{9,1},{13,5},{2,10},{6,14},... | collective-permute-start | bytes 24584 | tf_op jit(solution)/shard_map/ppermute | solution.py:446
  579.9 70.6 %collective-permute-start.69 = (bf16[256,2816]{1,0:T(8,128)(2,1)}, bf16[256,2816]{1,0:T(8,128)(2,1)}, u32[]{:S(2)}, u32[]{:S(2)}) collective-permute-start(bf16[256,2816]{1,0:T(8,128)(2,1)} %get-tuple-element.125), channel_id=1, source_target_pairs={{8,4},{12,8},{9,5},{13,9},{10,6},{14,10},{11,7},{15,11},{24,20},{2... | collective-permute-start | bytes 4325384 | tf_op jit(solution)/shard_map/ppermute | solution.py:454
  584.3 62.7 %collective-permute-start.45 = (bf16[256,1536]{1,0:T(8,128)(2,1)}, bf16[256,1536]{1,0:T(8,128)(2,1)}, u32[]{:S(2)}, u32[]{:S(2)}) collective-permute-start(bf16[256,1536]{1,0:T(8,128)(2,1)} %get-tuple-element.129), channel_id=1, source_target_pairs={{8,4},{12,8},{9,5},{13,9},{10,6},{14,10},{11,7},{15,11},{24,20},{2... | collective-permute-start | bytes 2359304 | tf_op jit(solution)/shard_map/ppermute | solution.py:454
  591.8 64.5 %collective-permute-start.55 = (bf16[256,512]{1,0:T(8,128)(2,1)S(1)}, bf16[256,512]{1,0:T(8,128)(2,1)S(1)}, u32[]{:S(2)}, u32[]{:S(2)}) collective-permute-start(bf16[256,512]{1,0:T(8,128)(2,1)S(1)} %get-tuple-element.145), channel_id=1, source_target_pairs={{0,4},{4,8},{8,12},{1,5},{5,9},{9,13},{2,6},{6,10},{10,14},{3,7},{... | collective-permute-start | bytes 786440 | tf_op jit(solution)/shard_map/ppermute | solution.py:454
  598.5 59.9 %collective-permute-start.58 = (bf16[256,512]{1,0:T(8,128)(2,1)S(1)}, bf16[256,512]{1,0:T(8,128)(2,1)S(1)}, u32[]{:S(2)}, u32[]{:S(2)}) collective-permute-start(bf16[256,512]{1,0:T(8,128)(2,1)S(1)} %add_convert_fusion.17), channel_id=1, source_target_pairs={{4,0},{8,4},{12,8},{5,1},{9,5},{13,9},{6,2},{10,6},{14,10},{7,3},{... | collective-permute-start | bytes 786440 | tf_op jit(solution)/shard_map/ppermute | solution.py:454
  600.4 61.9 %collective-permute-start.74 = (bf16[256,1408]{1,0:T(8,128)(2,1)}, bf16[256,1408]{1,0:T(8,128)(2,1)S(1)}, u32[]{:S(2)}, u32[]{:S(2)}) collective-permute-start(bf16[256,1408]{1,0:T(8,128)(2,1)} %get-tuple-element.132), channel_id=1, source_target_pairs={{0,4},{4,8},{8,12},{1,5},{5,9},{9,13},{2,6},{6,10},{10,14},{3,7},{... | collective-permute-start | bytes 2162696 | tf_op jit(solution)/shard_map/ppermute | solution.py:454
  658.3 41.2 %collective-permute-start.67 = (bf16[256,2816]{1,0:T(8,128)(2,1)S(1)}, bf16[256,2816]{1,0:T(8,128)(2,1)S(1)}, u32[]{:S(2)}, u32[]{:S(2)}) collective-permute-start(bf16[256,2816]{1,0:T(8,128)(2,1)S(1)} %copy-done.9), channel_id=1, source_target_pairs={{0,4},{4,8},{8,12},{1,5},{5,9},{9,13},{2,6},{6,10},{10,14},{3,7},{... | collective-permute-start | bytes 4325384 | tf_op jit(solution)/shard_map/ppermute | solution.py:454
  662.3 51.7 %collective-permute-start.70 = (bf16[256,2816]{1,0:T(8,128)(2,1)S(1)}, bf16[256,2816]{1,0:T(8,128)(2,1)S(1)}, u32[]{:S(2)}, u32[]{:S(2)}) collective-permute-start(bf16[256,2816]{1,0:T(8,128)(2,1)S(1)} %add_convert_fusion.3), channel_id=1, source_target_pairs={{4,0},{8,4},{12,8},{5,1},{9,5},{13,9},{6,2},{10,6},{14,10},{7,3},{... | collective-permute-start | bytes 4325384 | tf_op jit(solution)/shard_map/ppermute | solution.py:454
  (113 other events, 1901.7 us)
